TPU v7x, 512 devices: a whole 4x8x8 slice. The times are simulated.
512 devices in a mesh: replica: 64 (over y, z), tensor: 8 (over x, core).
Axes of the slice: x: 4, y: 8, z: 8, core: 2. Of those that a mesh axis runs over, the one named last changes fastest.
Arguments:
- query_proj: bfloat16 [65536, 8192], P('replica', 'tensor'), may hold values from -100 to 100
- key_proj: bfloat16 [65536, 1024], P('replica', 'tensor'), may hold values from -100 to 100
- value_proj: bfloat16 [65536, 1024], P('replica', 'tensor'), may hold values from -6 to 6
- traj_pages: int32 [64, 4], P('replica'), may hold values from 1 to 32, 64 in all within a row
- page_dest: int32 [64, 64], P('replica'), may hold values from 0 to 63, as said below
- page_table: int32 [64, 64], P('replica'), may hold values from 0 to 63, as said below
- query_gain: float32 [128], replicated, may hold values from 0.1 to 1.9
- key_gain: float32 [128], replicated, may hold values from 0.1 to 1.9
Outputs:
- attention: bfloat16 [65536, 8192], P(('replica', 'tensor'))
- page_pool: bfloat16 [4096, 16, 2048], P('replica', None, 'tensor')
Inputs may be any that keep to these rules, and one draw needn't show every extreme that they name: `page_dest`: each decoder group receives exactly 64 pages. At most 2 pages of one replica group go to one decoder group, and in every draw every replica group sends exactly 2 pages to some decoder group. `page_table`: the pages that reach one decoder group have distinct slots.
All inputs are finite; a program needn't handle non-finite values.
Results may differ from a plain program's by a relative error of at most 0.0061.
Values may be sent and summed in bfloat16 or wider, within the bound.
No kernel may reach another device: no remote copies, remote signals or barrier semaphores. Data moves between devices by JAX's collectives and lax.ppermute only.
A program may use at most 128 MiB of HBM per device.

v0:
```python
import math

import jax
import jax.numpy as jnp
from jax import lax
from jax.sharding import PartitionSpec as P

PAGE = 16


def positions(lengths, total_rows):
    token_index = jnp.arange(total_rows, dtype=jnp.int32)
    sizes = lengths * PAGE
    seq_ends = jnp.cumsum(sizes)
    seq_starts = seq_ends - sizes
    segment = jnp.sum((token_index[:, None] >= seq_ends[None, :]).astype(jnp.int32), axis=1)
    chosen = segment[:, None] == jnp.arange(lengths.shape[0], dtype=jnp.int32)[None, :]
    start_of = jnp.sum(jnp.where(chosen, seq_starts[None, :], 0), axis=1)
    return (segment, token_index - start_of)


def norm_rope(raw, gain_vec, places, head_size):
    row_count = raw.shape[0]
    head_count = raw.shape[1] // head_size
    entries = raw.astype(jnp.float32).reshape(row_count, head_count, head_size)
    mean_square = jnp.mean(entries * entries, axis=-1, keepdims=True)
    entries = entries * lax.rsqrt(mean_square + 1e-06) * gain_vec
    half_size = head_size // 2
    frequency = 1000000.0 ** (-(jnp.arange(half_size, dtype=jnp.float32) * 2.0 / head_size))
    angles = places.astype(jnp.float32)[:, None] * frequency[None, :]
    cosine = jnp.cos(angles)[:, None, :]
    sine_part = jnp.sin(angles)[:, None, :]
    first_half = entries[..., :half_size]
    second = entries[..., half_size:]
    rotated = jnp.concatenate(
        [first_half * cosine - second * sine_part, second * cosine + first_half * sine_part],
        axis=-1,
    )
    return rotated.astype(jnp.bfloat16).reshape(row_count, head_count * head_size)


def attend(query_rows, query_seg, query_idx, key_rows, value_rows, key_seg, key_idx, head_size):
    row_count = query_rows.shape[0]
    key_count = key_rows.shape[0]
    kv_heads = key_rows.shape[1] // head_size
    group_size = query_rows.shape[1] // head_size // kv_heads
    query_heads = query_rows.reshape(row_count, kv_heads, group_size, head_size)
    key_heads = key_rows.reshape(key_count, kv_heads, head_size)
    value_heads = value_rows.reshape(key_count, kv_heads, head_size)
    scores = jnp.einsum(
        "rkgd,skd->kgrs", query_heads, key_heads, preferred_element_type=jnp.float32
    ) * head_size ** (-0.5)
    allowed = (key_seg[None, :] == query_seg[:, None]) & (key_idx[None, :] <= query_idx[:, None])
    weights = jnp.where(allowed, jnp.exp(scores), 0.0)
    denominator = jnp.sum(weights, axis=-1)
    numerator = jnp.einsum(
        "kgrs,skd->rkgd",
        weights.astype(jnp.bfloat16),
        value_heads,
        preferred_element_type=jnp.float32,
    )
    normalized = numerator / jnp.transpose(denominator, (2, 0, 1))[..., None]
    return normalized.astype(jnp.bfloat16).reshape(row_count, kv_heads * group_size * head_size)


def ship_pages(key_ready, value_proj, dest_row, table_row, head_size):
    row_count = key_ready.shape[0]
    kv_heads = key_ready.shape[1] // head_size
    page_count = row_count // PAGE
    groups = lax.axis_size("replica")
    slots_per = max(2, page_count // groups + 1)
    row_width = kv_heads * 2 * head_size
    content = jnp.stack(
        [
            key_ready.reshape(row_count, kv_heads, head_size),
            value_proj.reshape(row_count, kv_heads, head_size),
        ],
        axis=2,
    )
    content = content.reshape(page_count, PAGE, row_width)
    page_order = jnp.arange(page_count, dtype=jnp.int32)
    same_dest = dest_row[:, None] == dest_row[None, :]
    earlier = page_order[None, :] < page_order[:, None]
    dest_rank = jnp.sum((same_dest & earlier).astype(jnp.int32), axis=1)
    target = dest_row * slots_per + dest_rank
    outbox = jnp.zeros((groups * slots_per, PAGE, row_width), jnp.bfloat16).at[target].set(content)
    labels = jnp.full((groups * slots_per,), -1, jnp.int32).at[target].set(table_row)
    arrived, slot_ids = (
        lax.all_to_all(outbox, "replica", split_axis=0, concat_axis=0, tiled=True),
        lax.all_to_all(labels, "replica", split_axis=0, concat_axis=0, tiled=True),
    )
    pool_slot = jnp.where(slot_ids >= 0, slot_ids, page_count)
    pool = jnp.zeros((page_count, PAGE, row_width), jnp.bfloat16)
    return pool.at[pool_slot].set(arrived, mode="drop")


def shards(
    query_proj, key_proj, value_proj, traj_pages, page_dest, page_table, query_gain, key_gain
):
    head_size = query_gain.shape[0]
    row_count = query_proj.shape[0]
    segment, places = positions(traj_pages[0], row_count)
    token_index = jnp.arange(row_count, dtype=jnp.int32)
    key_ready = norm_rope(key_proj, key_gain, places, head_size)
    pool = ship_pages(key_ready, value_proj, page_dest[0], page_table[0], head_size)
    block_rows = math.gcd(row_count, 128)
    block_total = row_count // block_rows
    query_ready = norm_rope(query_proj, query_gain, places, head_size)
    pieces = []
    for block_id in range(block_total):
        low_row = block_id * block_rows
        high_row = low_row + block_rows
        pieces.append(
            attend(
                query_ready[low_row:high_row],
                segment[low_row:high_row],
                token_index[low_row:high_row],
                key_ready[:high_row],
                value_proj[:high_row],
                segment[:high_row],
                token_index[:high_row],
                head_size,
            )
        )
    head_output = jnp.concatenate(pieces, axis=0)
    result = lax.all_to_all(head_output, "tensor", split_axis=0, concat_axis=1, tiled=True)
    return (result, pool)


def solution(mesh):
    in_specs = (
        P("replica", "tensor"),
        P("replica", "tensor"),
        P("replica", "tensor"),
        P("replica", None),
        P("replica", None),
        P("replica", None),
        P(),
        P(),
    )
    out_specs = (P(("replica", "tensor"), None), P("replica", None, "tensor"))
    return jax.shard_map(shards, mesh=mesh, in_specs=in_specs, out_specs=out_specs, check_vma=False)
```

profile of v0, /device:TPU:16, one launch (start us, length us, event | category | flops | bytes accessed | tf_op | source)
XLA Modules:
  0.0 140.0 jit_solution(16176587719496590482)
XLA Ops:
  0.6 0.9 convert_reduce_fusion
  2.2 0.9 scatter_custom_fusion
  3.9 16.5 %all-to-all-start.1 = ((s32[64,2,1]{1,2,0:T(1,128)}), s32[64,2,1]{1,2,0:T(1,128)S(1)}, u32[]{:S(2)}, u32[]{:S(2)}) async-start(s32[64,2,1]{1,2,0:T(1,128)} %bitcast.120), calls=%async_computation.1 | async-start | bytes 65536 | tf_op jit(solution)/shard_map/all_to_all | solution.py:90
  22.2 2.9 %copy.91 = bf16[1024,1024]{0,1:T(8,128)(2,1)S(1)} copy(bf16[1024,1024]{1,0:T(8,128)(2,1)} %param.8) | data formatting | bytes 4194304 | tf_op args[0]
  25.6 2.8 %copy.92 = f32[1024,8,128]{2,0,1:T(8,128)} copy(bf16[1024,8,128]{0,2,1:T(8,128)(2,1)S(1)} %bitcast.398) | data formatting | bytes 6291456 | tf_op jit(solution)/shard_map/reshape | solution.py:25
  28.7 1.9 %multiply_cosine_fusion = (f32[1024,64]{1,0:T(8,128)S(1)}, f32[1024,64]{1,0:T(8,128)S(1)}) fusion(f32[64]{0:T(128)S(1)} %negate_power_fusion, f32[1024]{0:T(1024)S(1)} %subtract_convert_fusion.1), kind=kLoop, calls=%fused_computation.82 | loop fusion | flops 65536 | bytes 528640 | tf_op jit(solution)/shard_map/cos | solution.py:31
  30.8 2.4 %fusion.99 = (bf16[1024,1,64]{2,0,1:T(8,128)(2,1)S(1)}, bf16[1024,1,64]{2,0,1:T(8,128)(2,1)S(1)}) fusion(f32[1024,1,128]{2,0,1:T(8,128)S(1)} %fusion.97, f32[64]{0:T(128)S(1)} %negate_power_fusion, f32[1024]{0:T(1024)S(1)} %subtract_convert_fusion.1), kind=kLoop, calls=%fused_computation.109 | loop fusion | flops 589824 | bytes 790784 | tf_op jit(solution)/shard_map/convert.11
  33.3 3.8 %multiply_multiply_fusion = f32[1024,8,128]{2,0,1:T(8,128)S(1)} fusion(f32[1024,8,128]{2,0,1:T(8,128)} %copy.92, f32[128]{0:T(128)S(1)} %copy-done.6, f32[1024,8]{0,1:T(8,128)S(1)} %add_rsqrt_fusion), kind=kLoop, calls=%fused_computation.6 | loop fusion | flops 2097152 | bytes 8421888 | tf_op jit(solution)/shard_map/mul | solution.py:27
  37.1 1.5 %add_convert_fusion = (bf16[1024,8,64]{2,0,1:T(8,128)(2,1)S(1)}, bf16[1024,8,64]{2,0,1:T(8,128)(2,1)S(1)}) fusion(f32[1024,8,128]{2,0,1:T(8,128)S(1)} %multiply_multiply_fusion, f32[1024,64]{1,0:T(8,128)S(1)} %get-tuple-element.11, f32[1024,64]{1,0:T(8,128)S(1)} %get-tuple-element.10), kind=kLoop, calls=%fused_computation.4 | loop fusion | flops 4194304 | bytes 6815744 | tf_op jit(solution)/shard_map/convert.10
  39.2 1.0 fusion.2
  40.3 0.9 fusion.4
  41.5 0.8 fusion.6
  46.3 1.2 fusion
  47.5 0.8 fusion.74
  52.3 2.6 %copy.109 = bf16[1024,1024]{1,0:T(8,128)(2,1)} copy(bf16[1024,1024]{0,1:T(8,128)(2,1)S(1)} %constant_dynamic-update-slice_fusion) | data formatting | bytes 4194304 | tf_op jit(solution)/shard_map/concatenate | solution.py:125
  54.9 4.3 %all-to-all-start = ((bf16[8,128,1024]{2,1,0:T(8,128)(2,1)}), bf16[8,128,1024]{2,1,0:T(8,128)(2,1)S(1)}, u32[]{:S(2)}, u32[]{:S(2)}) async-start(bf16[8,128,1024]{2,1,0:T(8,128)(2,1)} %bitcast.399), calls=%async_computation | async-start | bytes 4194304 | tf_op jit(solution)/shard_map/all_to_all | solution.py:126
  60.2 1.1 broadcast_in_dim.175
  61.3 7.1 %scatter_fusion = bf16[128,16,256]{2,1,0:T(8,128)(2,1)} fusion(bf16[128,16,256]{2,1,0:T(8,128)(2,1)} %broadcast_in_dim.175, s32[64]{0:T(128)S(1)} %fusion.167, bf16[64,16,256]{2,1,0:T(8,128)(2,1)S(1)} %reshape.594), kind=kCustom, calls=%fused_computation.1 | custom fusion | bytes 1573120 | tf_op jit(solution)/shard_map/scatter | solution.py:86
  68.4 18.0 %all-to-all-done = bf16[8,128,1024]{2,1,0:T(8,128)(2,1)S(1)} async-done(((bf16[8,128,1024]{2,1,0:T(8,128)(2,1)}), bf16[8,128,1024]{2,1,0:T(8,128)(2,1)S(1)}, u32[]{:S(2)}, u32[]{:S(2)}) %all-to-all-start) | async-done | bytes 2097184 | tf_op jit(solution)/shard_map/all_to_all | solution.py:126
  86.4 12.9 %all-to-all-start.2 = ((bf16[128,16,256]{2,1,0:T(8,128)(2,1)}), bf16[128,16,256]{2,1,0:T(8,128)(2,1)}, u32[]{:S(2)}, u32[]{:S(2)}) async-start(bf16[128,16,256]{2,1,0:T(8,128)(2,1)} %scatter_fusion), calls=%async_computation.2 | async-start | bytes 2097152 | tf_op jit(solution)/shard_map/all_to_all | solution.py:89
  100.7 2.4 %copy.110 = bf16[8,128,1024]{1,2,0:T(8,128)(2,1)} copy(bf16[8,128,1024]{2,1,0:T(8,128)(2,1)S(1)} %all-to-all-done) | data formatting | bytes 4194304 | tf_op jit(solution)/shard_map/all_to_all | solution.py:126
  103.1 4.1 %copy.113 = bf16[128,8192]{1,0:T(8,128)(2,1)} copy(bf16[128,8192]{0,1:T(8,128)(2,1)} %bitcast.400) | data formatting | bytes 4194304
  107.1 22.4 %all-to-all-done.2 = bf16[128,16,256]{2,1,0:T(8,128)(2,1)} async-done(((bf16[128,16,256]{2,1,0:T(8,128)(2,1)}), bf16[128,16,256]{2,1,0:T(8,128)(2,1)}, u32[]{:S(2)}, u32[]{:S(2)}) %all-to-all-start.2) | async-done | bytes 1048608 | tf_op jit(solution)/shard_map/all_to_all | solution.py:89
  129.5 9.6 %scatter_fusion.1 = bf16[64,16,256]{2,1,0:T(8,128)(2,1)S(1)} fusion(bf16[64,16,256]{2,1,0:T(8,128)(2,1)S(1)} %broadcast_in_dim.172, s32[128]{0:T(128)S(1)} %fusion.168, bf16[128,16,256]{2,1,0:T(8,128)(2,1)} %all-to-all-done.2), kind=kCustom, calls=%fused_computation.2 | custom fusion | bytes 3146240 | tf_op jit(solution)/shard_map/scatter | solution.py:94
  (92 shorter events, 16.0 us)
Async XLA Ops:
  3.9 51.0 %all-to-all-start.1 = ((s32[64,2,1]{1,2,0:T(1,128)}), s32[64,2,1]{1,2,0:T(1,128)S(1)}, u32[]{:S(2)}, u32[]{:S(2)}) async-start(s32[64,2,1]{1,2,0:T(1,128)} %bitcast.120), calls=%async_computation.1 | async-start | bytes 65536 | tf_op jit(solution)/shard_map/all_to_all | solution.py:90
  22.0 3.1 %copy-start.3 = (s32[1024]{0:T(1024)}, s32[1024]{0:T(1024)S(1)}, u32[]{:S(2)}) copy-start(s32[1024]{0:T(1024)S(1)} %iota.52) | copy-start | bytes 12292
  22.0 3.0 %copy-start.4 = (s32[1024]{0:T(1024)}, s32[1024]{0:T(1024)S(1)}, u32[]{:S(2)}) copy-start(s32[1024]{0:T(1024)S(1)} %iota.51) | copy-start | bytes 12292
  22.1 3.0 %copy-start.5 = (s32[1024]{0:T(1024)}, s32[1024]{0:T(1024)S(1)}, u32[]{:S(2)}) copy-start(s32[1024]{0:T(1024)S(1)} %iota.50) | copy-start | bytes 12292
  25.6 2.9 %copy-start.1 = (bf16[1024,128]{1,0:T(8,128)(2,1)S(1)}, bf16[1024,128]{1,0:T(8,128)(2,1)}, u32[]{:S(2)}) copy-start(bf16[1024,128]{1,0:T(8,128)(2,1)} %param.9) | copy-start | bytes 786436
  25.6 5.0 %copy-start.7 = (f32[128]{0:T(128)S(1)}, f32[128]{0:T(128)}, u32[]{:S(2)}) copy-start(f32[128]{0:T(128)} %param.15) | copy-start | bytes 1540
  28.4 4.9 %copy-start.6 = (f32[128]{0:T(128)S(1)}, f32[128]{0:T(128)}, u32[]{:S(2)}) copy-start(f32[128]{0:T(128)} %param.14) | copy-start | bytes 1540
  41.4 0.8 slice-start
  42.5 0.7 slice-start.1
  43.4 0.7 slice-start.2
  44.8 1.0 copy-start.2
  54.9 31.5 %all-to-all-start = ((bf16[8,128,1024]{2,1,0:T(8,128)(2,1)}), bf16[8,128,1024]{2,1,0:T(8,128)(2,1)S(1)}, u32[]{:S(2)}, u32[]{:S(2)}) async-start(bf16[8,128,1024]{2,1,0:T(8,128)(2,1)} %bitcast.399), calls=%async_computation | async-start | bytes 4194304 | tf_op jit(solution)/shard_map/all_to_all | solution.py:126
  86.4 43.1 %all-to-all-start.2 = ((bf16[128,16,256]{2,1,0:T(8,128)(2,1)}), bf16[128,16,256]{2,1,0:T(8,128)(2,1)}, u32[]{:S(2)}, u32[]{:S(2)}) async-start(bf16[128,16,256]{2,1,0:T(8,128)(2,1)} %scatter_fusion), calls=%async_computation.2 | async-start | bytes 2097152 | tf_op jit(solution)/shard_map/all_to_all | solution.py:89
  139.2 0.8 copy-start
where the time goes:
time: 141 us; the launch traced here: 140 us
  waiting for transfers between devices  40.3 us (29%)
  local copies, waits for them, and re-layouts  38.1 us (27%)
  starting transfers between devices  33.7 us (24%)
  other arithmetic  16.3 us (12%)
  matrix products  10.3 us (7%)
    all_to_all x1, waiting for transfers between devices, ship_pages(): lax.all_to_all(outbox, 'replica', split_axis=0, concat_axis=0, tiled=True)  22.4 us
    all_to_all x1, waiting for transfers between devices, shards(): lax.all_to_all(head_output, 'tensor', split_axis=0, concat_axis=1, tiled=...  18 us
    all_to_all x1, starting transfers between devices, ship_pages(): lax.all_to_all(labels, 'replica', split_axis=0, concat_axis=0, tiled=True)  16.5 us
    all_to_all x1, starting transfers between devices, ship_pages(): lax.all_to_all(outbox, 'replica', split_axis=0, concat_axis=0, tiled=True)  12.9 us
    scatter x1, local copies, waits for them, and re-layouts, ship_pages(): return pool.at[pool_slot].set(arrived, mode='drop')  9.64 us
    unnamed x25, local copies, waits for them, and re-layouts  9.11 us
    scatter x1, local copies, waits for them, and re-layouts, ship_pages(): jnp.zeros((groups * slots_per, PAGE, row_width), jnp.bfloat16).at[target]  7.12 us
    dot_general x8, matrix products, attend(): jnp.einsum('rkgd,skd->kgrs', query_heads, key_heads, preferred_element_ty...  6.1 us
  transfers between devices with their start and end apart: 3, of which 2 were waited for; matrix products, arithmetic and copies ran while one was open for 36% of the time, Pallas kernels for 0%

commit v1 on v0

v1 whole, which is shorter than its diff:
```python
import functools

import jax
import jax.numpy as jnp
import numpy as np
from jax import lax
from jax.experimental import pallas as pl
from jax.experimental.pallas import tpu as pltpu
from jax.sharding import PartitionSpec as P

PAGE = 16
HD = 128
HALF = HD // 2
ROWS = 1024
BLOCK = 128
WINDOW = 256
PAGES = ROWS // PAGE
MOST = 32
HEADS = 8
HALF_ROWS = HEADS // 2 * BLOCK
GROUPS = 64
SLOTS = 2 * GROUPS
CHIPS = 4
BATCH = 8
EPS = 1e-06
LABEL_ROWS = 8
LETTER = 4 * PAGE + LABEL_ROWS
NEG = -1e30
SCALE = HD**-0.5 * np.log2(np.e)
STEPS = ((1, 0), (3, 0), (2, 0), (1, 1), (3, 1), (2, 1), (0, 1))


def rope_tables():
    frequency = 1000000.0 ** (-(np.arange(HALF) * 2.0 / HD))
    places = np.concatenate([np.arange(MOST) * PAGE, np.arange(PAGE)])
    angles = places[:, None] * frequency[None, :]
    cosine = np.concatenate([np.cos(angles)] * 2, axis=1)
    sine = np.concatenate([-np.sin(angles), np.sin(angles)], axis=1)
    return cosine.astype(np.float32), sine.astype(np.float32)


def seq_ends(traj_ref):
    first = traj_ref[0]
    second = first + traj_ref[1]
    return first, second, second + traj_ref[2]


def start_of(ends, place):
    low = jnp.int32(0)
    for end in ends:
        low = jnp.where(place >= end, end, low)
    return low


def page_rope(cos_ref, sin_ref, index):
    cos_row = cos_ref[pl.ds(index, 1), :]
    sin_row = sin_ref[pl.ds(index, 1), :]
    cos_in = cos_ref[MOST : MOST + PAGE, :]
    sin_in = sin_ref[MOST : MOST + PAGE, :]
    return cos_row * cos_in - sin_row * sin_in, sin_row * cos_in + cos_row * sin_in


def prep_kernel(
    traj_ref, dest_ref, table_ref, key_ref, value_ref, gain_ref, cos_ref, sin_ref,
    ready_ref, outbox_ref, slot_ref,
):
    ends = seq_ends(traj_ref)
    for index in range(SLOTS):
        slot_ref[index] = -1
    gain = gain_ref[...]
    gain_turned = pltpu.roll(gain, HALF, 1)
    for page in range(PAGES):
        rows = pl.ds(page * PAGE, PAGE)
        cosine, sine = page_rope(cos_ref, sin_ref, page - start_of(ends, page))
        entries = key_ref[rows, :].astype(jnp.float32)
        mean_square = jnp.mean(entries * entries, axis=-1, keepdims=True)
        turned = pltpu.roll(entries, HALF, 1)
        mixed = entries * (cosine * gain) + turned * (sine * gain_turned)
        ready = (mixed * lax.rsqrt(mean_square + EPS)).astype(jnp.bfloat16)
        ready_ref[rows, :] = ready
        dest = dest_ref[page]
        rank = jnp.where(slot_ref[dest * 2] >= 0, 1, 0)
        slot_ref[dest * 2 + rank] = table_ref[page]
        outbox_ref[dest, pl.ds(pl.multiple_of(rank * 2 * PAGE, PAGE), PAGE), :] = ready
        outbox_ref[dest, pl.ds(pl.multiple_of(rank * 2 * PAGE + PAGE, PAGE), PAGE), :] = value_ref[
            rows, :
        ]
    odd = lax.broadcasted_iota(jnp.int32, (LABEL_ROWS, HD), 1) % 2
    for dest in range(GROUPS):
        slots = jnp.where(odd == 0, slot_ref[dest * 2], slot_ref[dest * 2 + 1])
        outbox_ref[dest, LETTER - LABEL_ROWS :, :] = slots.astype(jnp.float32).astype(jnp.bfloat16)


def attend_kernel(
    block_ref, traj_ref, query_ref, key_ref, value_ref, gain_ref, cos_ref, sin_ref, *refs
):
    for index, out_ref in enumerate(refs[:-4]):
        attend_block(
            block_ref[index], traj_ref, query_ref, key_ref, value_ref, gain_ref, cos_ref, sin_ref,
            out_ref, *refs[-4:],
        )


def attend_block(
    block, traj_ref, query_ref, key_ref, value_ref, gain_ref, cos_ref, sin_ref, out_ref,
    cos_rows, sin_rows, ready, total,
):
    ends = seq_ends(traj_ref)
    gain = gain_ref[...] * SCALE
    gain_turned = pltpu.roll(gain, HALF, 1)
    for page in range(BLOCK // PAGE):
        place = block * (BLOCK // PAGE) + page
        cosine, sine = page_rope(cos_ref, sin_ref, place - start_of(ends, place))
        cos_rows[page * PAGE : (page + 1) * PAGE, :] = cosine * gain
        sin_rows[page * PAGE : (page + 1) * PAGE, :] = sine * gain_turned
    ones = jnp.ones((WINDOW, HD), jnp.bfloat16)
    lane = lax.broadcasted_iota(jnp.int32, (HD, HD), 1)
    turn = lax.broadcasted_iota(jnp.int32, (HD, HD), 0) == (lane + HALF) % HD
    turn = jnp.where(turn, 1.0, 0.0).astype(jnp.bfloat16)
    rows = pl.ds(pl.multiple_of(block * BLOCK, BLOCK), BLOCK)
    for head in range(HEADS):
        raw = query_ref[rows, head * HD : (head + 1) * HD]
        entries = raw.astype(jnp.float32)
        square = entries * entries
        upper = square.astype(jnp.bfloat16)
        lower = (square - upper.astype(jnp.float32)).astype(jnp.bfloat16)
        total_square = jnp.dot(
            jnp.concatenate([upper, lower], axis=1), ones, preferred_element_type=jnp.float32
        )
        turned = jnp.dot(raw, turn, preferred_element_type=jnp.float32)
        mixed = entries * cos_rows[...] + turned * sin_rows[...]
        scaled = mixed * lax.rsqrt(total_square * (1.0 / HD) + EPS)
        ready[head * BLOCK : (head + 1) * BLOCK, :] = scaled.astype(jnp.bfloat16)

    low = block * BLOCK
    high = low + BLOCK
    first = start_of(ends, block * (BLOCK // PAGE)) * PAGE
    windows = (high - first + WINDOW - 1) // WINDOW
    base = jnp.maximum(high - windows * WINDOW, 0)
    token = low + lax.broadcasted_iota(jnp.int32, (BLOCK, WINDOW), 0)
    begin = jnp.zeros((BLOCK, WINDOW), jnp.int32)
    for end in ends:
        begin = jnp.where(token >= end * PAGE, end * PAGE, begin)
    column = lax.broadcasted_iota(jnp.int32, (BLOCK, WINDOW), 1)

    def window(index, add):
        offset = pl.multiple_of(base + index * WINDOW, BLOCK)
        keys = key_ref[pl.ds(offset, WINDOW), :]
        values = jnp.concatenate([value_ref[pl.ds(offset, WINDOW), :], ones], axis=1)
        other = offset + column
        bias = jnp.where((other >= begin) & (other <= token), 0.0, NEG)
        for part in range(2):
            part_rows = slice(part * HALF_ROWS, (part + 1) * HALF_ROWS)
            scores = lax.dot_general(
                ready[part_rows, :], keys, (((1,), (1,)), ((), ())), preferred_element_type=jnp.float32
            )
            biased = scores.reshape(HEADS // 2, BLOCK, WINDOW) + bias[None]
            weights = jnp.exp2(biased).astype(jnp.bfloat16).reshape(HALF_ROWS, WINDOW)
            summed = jnp.dot(weights, values, preferred_element_type=jnp.float32)
            if add:
                total[part_rows, :] += summed
            else:
                total[part_rows, :] = summed

    window(0, False)
    lax.fori_loop(1, windows, lambda index, carry: (window(index, True), carry)[1], 0)
    for head in range(HEADS):
        head_rows = slice(head * BLOCK, (head + 1) * BLOCK)
        out_ref[:, head * HD : (head + 1) * HD] = (
            total[head_rows, :HD] / total[head_rows, HD:]
        ).astype(jnp.bfloat16)


def assemble_kernel(source_ref, *refs):
    count = (len(refs) - 3) // 2
    pieces, out_ref = refs[:count], refs[count]
    held, in_sems, out_sems = refs[count + 1 : count + 1 + count], refs[-2], refs[-1]
    loads, stores = [], []
    for index, piece in enumerate(pieces):
        width = piece.shape[1]
        columns = pl.ds(pl.multiple_of(source_ref[index] * width, width), width)
        loads.append(pltpu.make_async_copy(piece, held[index], in_sems.at[index]))
        stores.append(
            pltpu.make_async_copy(held[index], out_ref.at[:, columns], out_sems.at[index])
        )
    for load in loads:
        load.start()
    for load, store in zip(loads, stores):
        load.wait()
        store.start()
    for store in stores:
        store.wait()


def pool_kernel(arrived_ref, pool_ref, label_ref, slot_ref, place_ref, sem):
    lane = lax.broadcasted_iota(jnp.int32, (LABEL_ROWS, HD), 1) // 2
    labels = jnp.zeros((LABEL_ROWS, HD), jnp.float32)
    for group in range(GROUPS):
        mine = arrived_ref[group, LETTER - LABEL_ROWS :, :].astype(jnp.float32)
        labels = jnp.where(lane == group, mine, labels)
    label_ref[...] = labels.astype(jnp.int32)
    fetch = pltpu.make_async_copy(label_ref, slot_ref, sem)
    fetch.start()
    fetch.wait()
    for index in range(SLOTS):
        slot = slot_ref[0, index]
        place_ref[jnp.where(slot < 0, PAGES, slot)] = index
    for slot in range(PAGES):
        index = place_ref[slot]
        group, row = index // 2, index % 2 * (2 * PAGE)
        for half in range(2):
            rows = pl.ds(pl.multiple_of(row + half * PAGE, PAGE), PAGE)
            pool_ref[slot, :, half * HD : (half + 1) * HD] = arrived_ref[group, rows, :]


VMEM = pl.BlockSpec(memory_space=pltpu.VMEM)
SMEM = pl.BlockSpec(memory_space=pltpu.SMEM)
ANY = pl.BlockSpec(memory_space=pl.ANY)
ATTEND_VMEM = 12 << 20
PARAMS = pltpu.CompilerParams(vmem_limit_bytes=63 << 20)


def cost(flops, moved):
    return pl.CostEstimate(flops=flops, bytes_accessed=moved, transcendentals=0)


def prep(traj, dest, table, key_proj, value_proj, gain, cosine, sine):
    return pl.pallas_call(
        prep_kernel,
        out_shape=(
            jax.ShapeDtypeStruct((ROWS, HD), jnp.bfloat16),
            jax.ShapeDtypeStruct((GROUPS, LETTER, HD), jnp.bfloat16),
        ),
        in_specs=[SMEM] * 3 + [VMEM] * 5,
        out_specs=(VMEM, VMEM),
        scratch_shapes=[pltpu.SMEM((SLOTS,), jnp.int32)],
        compiler_params=PARAMS,
        cost_estimate=cost(10**6, 4 << 20),
        name="prep",
    )(traj, dest, table, key_proj, value_proj, gain, cosine, sine)


def attend(blocks, traj, query_proj, ready, value_proj, gain, cosine, sine):
    return pl.pallas_call(
        attend_kernel,
        out_shape=[jax.ShapeDtypeStruct((BLOCK, HEADS * HD), jnp.bfloat16)] * len(blocks),
        in_specs=[SMEM] * 2 + [VMEM] * 6,
        out_specs=[VMEM] * len(blocks),
        scratch_shapes=[
            pltpu.VMEM((BLOCK, HD), jnp.float32),
            pltpu.VMEM((BLOCK, HD), jnp.float32),
            pltpu.VMEM((HEADS * BLOCK, HD), jnp.bfloat16),
            pltpu.VMEM((HEADS * BLOCK, 2 * HD), jnp.float32),
        ],
        compiler_params=pltpu.CompilerParams(vmem_limit_bytes=ATTEND_VMEM),
        cost_estimate=cost(len(blocks) * 400 * 10**6, 4 << 20),
        name="attend",
    )(jnp.stack(blocks), traj, query_proj, ready, value_proj, gain, cosine, sine)


def assemble(sources, pieces):
    rows, width = pieces[0].shape
    return pl.pallas_call(
        assemble_kernel,
        out_shape=jax.ShapeDtypeStruct((rows, width * len(pieces)), jnp.bfloat16),
        in_specs=[SMEM] + [ANY] * len(pieces),
        out_specs=ANY,
        scratch_shapes=[pltpu.VMEM(piece.shape, piece.dtype) for piece in pieces]
        + [pltpu.SemaphoreType.DMA((len(pieces),))] * 2,
        compiler_params=PARAMS,
        cost_estimate=cost(10**6, 4 << 20),
        name="assemble",
    )(sources, *pieces)


def fill_pool(arrived):
    return pl.pallas_call(
        pool_kernel,
        out_shape=jax.ShapeDtypeStruct((PAGES, PAGE, 2 * HD), jnp.bfloat16),
        in_specs=[VMEM],
        out_specs=VMEM,
        scratch_shapes=[
            pltpu.VMEM((LABEL_ROWS, HD), jnp.int32),
            pltpu.SMEM((LABEL_ROWS, HD), jnp.int32),
            pltpu.SMEM((PAGES + 1,), jnp.int32),
            pltpu.SemaphoreType.DMA,
        ],
        compiler_params=PARAMS,
        cost_estimate=cost(10**6, 2 << 20),
        name="pool",
    )(arrived)


def shards(
    query_proj, key_proj, value_proj, traj_pages, page_dest, page_table, query_gain, key_gain
):
    cosine, sine = (jnp.asarray(table) for table in rope_tables())
    traj, dest, table = traj_pages[0], page_dest[0], page_table[0]
    query_gain, key_gain = query_gain[None, :], key_gain[None, :]
    ready, outbox = prep(traj, dest, table, key_proj, value_proj, key_gain, cosine, sine)
    arrived = lax.all_to_all(outbox, "replica", split_axis=0, concat_axis=0, tiled=True)

    me = lax.axis_index("tensor")
    chip, core = me // 2, me % 2
    targets = [(chip + step) % CHIPS * 2 + (core ^ flip) for step, flip in STEPS] + [me]
    sources = [(chip - step + CHIPS) % CHIPS * 2 + (core ^ flip) for step, flip in STEPS] + [me]
    pieces = []
    for begin in range(0, len(targets), BATCH):
        pieces += attend(
            targets[begin : begin + BATCH], traj, query_proj, ready, value_proj, query_gain, cosine, sine
        )
    for index, (step, flip) in enumerate(STEPS):
        pairs = [
            (x * 2 + c, (x + step) % CHIPS * 2 + (c ^ flip)) for x in range(CHIPS) for c in range(2)
        ]
        pieces[index] = lax.ppermute(pieces[index], "tensor", pairs)
    return assemble(jnp.stack(sources), pieces), fill_pool(arrived)


def solution(mesh):
    in_specs = (
        P("replica", "tensor"),
        P("replica", "tensor"),
        P("replica", "tensor"),
        P("replica", None),
        P("replica", None),
        P("replica", None),
        P(),
        P(),
    )
    out_specs = (P(("replica", "tensor"), None), P("replica", None, "tensor"))
    return jax.shard_map(shards, mesh=mesh, in_specs=in_specs, out_specs=out_specs, check_vma=False)
```

time: 141 us -> 70.5 us (0.50)
  the two profiles are of different devices: /device:TPU:16 before, /device:TPU:19 now
where the time goes in v1:
time: 70.5 us; the launch traced here: 70 us
  starting transfers between devices  38.1 us (54%)
  Pallas kernels  20.3 us (29%)
  waiting for transfers between devices  7.14 us (10%)
  local copies, waits for them, and re-layouts  3.52 us (5%)
  between operations  0.98 us (1%)
    ppermute x7, starting transfers between devices, shards(): pieces[index] = lax.ppermute(pieces[index], 'tensor', pairs)  21.9 us
    all_to_all x1, starting transfers between devices, shards(): lax.all_to_all(outbox, 'replica', split_axis=0, concat_axis=0, tiled=True)  16.2 us
    pallas_call x1, Pallas kernels, attend(): pl.pallas_call(attend_kernel, out_shape=[jax.ShapeDtypeStruct((BLOCK, HEA...  10.5 us
    ppermute x7, waiting for transfers between devices, shards(): pieces[index] = lax.ppermute(pieces[index], 'tensor', pairs)  7.14 us
    pallas_call x1, Pallas kernels, fill_pool(): pl.pallas_call(pool_kernel, out_shape=jax.ShapeDtypeStruct((PAGES, PAGE,...  3.47 us
    pallas_call x1, Pallas kernels, prep(): pl.pallas_call(prep_kernel, out_shape=(jax.ShapeDtypeStruct((ROWS, HD), j...  3.25 us
    pallas_call x1, Pallas kernels, assemble(): pl.pallas_call(assemble_kernel, out_shape=jax.ShapeDtypeStruct((rows, wid...  3.06 us
    unnamed x30, local copies, waits for them, and re-layouts  2.82 us
  transfers between devices with their start and end apart: 8, of which 2 were waited for; matrix products, arithmetic and copies ran while one was open for 1% of the time, Pallas kernels for 19%

profile of v1, /device:TPU:19, one launch (start us, length us, event | category | flops | bytes accessed | tf_op | source)
XLA Modules:
  0.0 70.0 jit_solution(4973521588678199131)
XLA Ops:
  0.6 0.0 copy-start.2
  0.6 0.0 copy-start.3
  0.7 3.3 %prep.1 = (bf16[1024,128]{1,0:T(8,128)(2,1)}, bf16[64,72,128]{2,1,0:T(8,128)(2,1)}) custom-call(s32[4]{0:T(128)} %bitcast.14, s32[64]{0:T(128)} %bitcast.17, s32[64]{0:T(128)} %bitcast.18, bf16[1024,128]{1,0:T(8,128)(2,1)} %key_ref.1, bf16[1024,128]{1,0:T(8,128)(2,1)} %value_ref.3, f32[1,128]{1,0:T(1,128)} %bitcast.19, f32[48,128]{1,0:T(8,128)} %constant.90.clone.cos_ref, ...), custom_call_target="tpu_custom_call" | custom-call | flops 1000000 | bytes 4194304 | tf_op jit(solution)/shard_map/prep/pallas_call | solution.py:228
  3.9 16.2 %all-to-all-start = ((bf16[64,72,128]{2,1,0:T(8,128)(2,1)}), bf16[64,72,128]{2,1,0:T(8,128)(2,1)}, u32[]{:S(2)}, u32[]{:S(2)}) async-start(bf16[64,72,128]{2,1,0:T(8,128)(2,1)} %get-tuple-element.21), calls=%async_computation | async-start | bytes 2359296 | tf_op jit(solution)/shard_map/all_to_all | solution.py:301
  20.3 0.1 stack.50.block_ref
  20.4 10.5 %attend.1 = (bf16[128,1024]{1,0:T(8,128)(2,1)S(1)}, bf16[128,1024]{1,0:T(8,128)(2,1)S(1)}, bf16[128,1024]{1,0:T(8,128)(2,1)}, bf16[128,1024]{1,0:T(8,128)(2,1)},...) custom-call(s32[8]{0:T(128)S(1)} %stack.50.block_ref, ...), custom_call_target="tpu_custom_call" | custom-call | flops 3200000000 | bytes 4194304 | tf_op jit(solution)/shard_map/attend/pallas_call | solution.py:244
  30.9 0.7 %copy-done = bf16[128,1024]{1,0:T(8,128)(2,1)} copy-done((bf16[128,1024]{1,0:T(8,128)(2,1)}, bf16[128,1024]{1,0:T(8,128)(2,1)S(1)}, u32[]{:S(2)}) %copy-start) | copy-done | bytes 262168
  31.6 3.1 %collective-permute-start = (bf16[128,1024]{1,0:T(8,128)(2,1)S(1)}, bf16[128,1024]{1,0:T(8,128)(2,1)S(1)}, u32[]{:S(2)}, u32[]{:S(2)}) collective-permute-start(bf16[128,1024]{1,0:T(8,128)(2,1)S(1)} %get-tuple-element.13), channel_id=1, source_target_pairs={{0,2},{1,3},{2,4},{3,5},{4,6},{5,7},{6,0},{7,1},{8,10},{9,11},{10,... | collective-permute-start | bytes 786440 | tf_op jit(solution)/shard_map/ppermute | solution.py:316
  34.7 2.2 %collective-permute-start.1 = (bf16[128,1024]{1,0:T(8,128)(2,1)S(1)}, bf16[128,1024]{1,0:T(8,128)(2,1)S(1)}, u32[]{:S(2)}, u32[]{:S(2)}) collective-permute-start(bf16[128,1024]{1,0:T(8,128)(2,1)S(1)} %get-tuple-element.14), channel_id=1, source_target_pairs={{0,6},{1,7},{2,0},{3,1},{4,2},{5,3},{6,4},{7,5},{8,14},{9,15},{10,... | collective-permute-start | bytes 786440 | tf_op jit(solution)/shard_map/ppermute | solution.py:316
  36.9 3.7 %collective-permute-start.2 = (bf16[128,1024]{1,0:T(8,128)(2,1)}, bf16[128,1024]{1,0:T(8,128)(2,1)S(1)}, u32[]{:S(2)}, u32[]{:S(2)}) collective-permute-start(bf16[128,1024]{1,0:T(8,128)(2,1)} %get-tuple-element.15), channel_id=1, source_target_pairs={{0,4},{1,5},{2,6},{3,7},{4,0},{5,1},{6,2},{7,3},{8,12},{9,13},{10,... | collective-permute-start | bytes 786440 | tf_op jit(solution)/shard_map/ppermute | solution.py:316
  40.6 4.7 %collective-permute-start.3 = (bf16[128,1024]{1,0:T(8,128)(2,1)}, bf16[128,1024]{1,0:T(8,128)(2,1)S(1)}, u32[]{:S(2)}, u32[]{:S(2)}) collective-permute-start(bf16[128,1024]{1,0:T(8,128)(2,1)} %get-tuple-element.16), channel_id=1, source_target_pairs={{0,3},{1,2},{2,5},{3,4},{4,7},{5,6},{6,1},{7,0},{8,11},{9,10},{10,... | collective-permute-start | bytes 786440 | tf_op jit(solution)/shard_map/ppermute | solution.py:316
  45.3 2.3 %collective-permute-start.4 = (bf16[128,1024]{1,0:T(8,128)(2,1)}, bf16[128,1024]{1,0:T(8,128)(2,1)S(1)}, u32[]{:S(2)}, u32[]{:S(2)}) collective-permute-start(bf16[128,1024]{1,0:T(8,128)(2,1)} %get-tuple-element.17), channel_id=1, source_target_pairs={{0,7},{1,6},{2,1},{3,0},{4,3},{5,2},{6,5},{7,4},{8,15},{9,14},{10,... | collective-permute-start | bytes 786440 | tf_op jit(solution)/shard_map/ppermute | solution.py:316
  47.6 0.0 collective-permute-done.refs_0_
  47.6 3.6 %collective-permute-start.5 = (bf16[128,1024]{1,0:T(8,128)(2,1)S(1)}, bf16[128,1024]{1,0:T(8,128)(2,1)S(1)}, u32[]{:S(2)}, u32[]{:S(2)}) collective-permute-start(bf16[128,1024]{1,0:T(8,128)(2,1)S(1)} %get-tuple-element.18), channel_id=1, source_target_pairs={{0,5},{1,4},{2,7},{3,6},{4,1},{5,0},{6,3},{7,2},{8,13},{9,12},{10,... | collective-permute-start | bytes 786440 | tf_op jit(solution)/shard_map/ppermute | solution.py:316
  51.2 0.7 %copy-done.9 = bf16[128,1024]{1,0:T(8,128)(2,1)} copy-done((bf16[128,1024]{1,0:T(8,128)(2,1)}, bf16[128,1024]{1,0:T(8,128)(2,1)S(1)}, u32[]{:S(2)}) %copy-start.9) | copy-done | bytes 262168
  51.9 2.4 %collective-permute-start.6 = (bf16[128,1024]{1,0:T(8,128)(2,1)S(1)}, bf16[128,1024]{1,0:T(8,128)(2,1)S(1)}, u32[]{:S(2)}, u32[]{:S(2)}) collective-permute-start(bf16[128,1024]{1,0:T(8,128)(2,1)S(1)} %get-tuple-element.19), channel_id=1, source_target_pairs={{0,1},{1,0},{2,3},{3,2},{4,5},{5,4},{6,7},{7,6},{8,9},{9,8},{10,11... | collective-permute-start | bytes 786440 | tf_op jit(solution)/shard_map/ppermute | solution.py:316
  54.3 0.6 stack.48.source_ref
  55.0 0.0 collective-permute-done.2.refs_2_
  55.0 2.1 %collective-permute-done.4.refs_4_ = bf16[128,1024]{1,0:T(8,128)(2,1)S(1)} collective-permute-done((bf16[128,1024]{1,0:T(8,128)(2,1)}, bf16[128,1024]{1,0:T(8,128)(2,1)S(1)}, u32[]{:S(2)}, u32[]{:S(2)}) %collective-permute-start.4) | collective-permute-done | bytes 262176 | tf_op jit(solution)/shard_map/ppermute | solution.py:316
  57.1 5.0 %collective-permute-done.5.refs_5_ = bf16[128,1024]{1,0:T(8,128)(2,1)S(1)} collective-permute-done((bf16[128,1024]{1,0:T(8,128)(2,1)S(1)}, bf16[128,1024]{1,0:T(8,128)(2,1)S(1)}, u32[]{:S(2)}, u32[]{:S(2)}) %collective-permute-start.5) | collective-permute-done | bytes 262176 | tf_op jit(solution)/shard_map/ppermute | solution.py:316
  62.1 0.7 copy-done.13
  62.8 0.7 copy-done.14
  63.5 3.1 %assemble.1 = bf16[128,8192]{1,0:T(8,128)(2,1)} custom-call(s32[8]{0:T(128)} %stack.48.source_ref, bf16[128,1024]{1,0:T(8,128)(2,1)} %copy-done.8, bf16[128,1024]{1,0:T(8,128)(2,1)} %copy-done.9, bf16[128,1024]{1,0:T(8,128)(2,1)} %copy-done.10, bf16[128,1024]{1,0:T(8,128)(2,1)} %copy-done.11, bf16[128,1024]{1,0:T(8,128)(2,1)} %copy-done.12, ...), custom_call_target="tpu_custom_call" | custom-call | flops 1000000 | bytes 4194304 | tf_op jit(solution)/shard_map/assemble/pallas_call | solution.py:263
  66.6 3.5 %pool.1 = bf16[64,16,256]{2,1,0:T(8,128)(2,1)} custom-call(bf16[64,72,128]{2,1,0:T(8,128)(2,1)} %all-to-all-done.arrived_ref), custom_call_target="tpu_custom_call" | custom-call | flops 1000000 | bytes 2097152 | tf_op jit(solution)/shard_map/pool/pallas_call | solution.py:277
  (28 shorter events, 0.1 us)
Async XLA Ops:
  0.6 19.7 %copy-start.2 = (f32[48,128]{1,0:T(8,128)S(1)}, f32[48,128]{1,0:T(8,128)}, u32[]{:S(2)}) copy-start(f32[48,128]{1,0:T(8,128)} %constant.91.clone.sin_ref) | copy-start | bytes 73732
  0.6 19.7 %copy-start.3 = (f32[48,128]{1,0:T(8,128)S(1)}, f32[48,128]{1,0:T(8,128)}, u32[]{:S(2)}) copy-start(f32[48,128]{1,0:T(8,128)} %constant.90.clone.cos_ref) | copy-start | bytes 73732
  0.7 19.7 %copy-start.1 = (bf16[1024,128]{1,0:T(8,128)(2,1)S(1)}, bf16[1024,128]{1,0:T(8,128)(2,1)}, u32[]{:S(2)}) copy-start(bf16[1024,128]{1,0:T(8,128)(2,1)} %value_ref.3) | copy-start | bytes 786436
  0.7 19.7 %copy-start.4 = (s32[1,4]{1,0:T(1,128)S(1)}, s32[1,4]{1,0:T(1,128)}, u32[]{:S(2)}) copy-start(s32[1,4]{1,0:T(1,128)} %param.13) | copy-start | bytes 52
  0.7 19.7 %copy-start.7 = (f32[128]{0:T(128)S(1)}, f32[128]{0:T(128)}, u32[]{:S(2)}) copy-start(f32[128]{0:T(128)} %param.16) | copy-start | bytes 1540
  3.9 16.4 %copy-start.5 = (bf16[1024,1024]{1,0:T(8,128)(2,1)S(1)}, bf16[1024,1024]{1,0:T(8,128)(2,1)}, u32[]{:S(2)}) copy-start(bf16[1024,1024]{1,0:T(8,128)(2,1)} %query_ref.1) | copy-start | bytes 6291460
  3.9 16.4 %copy-start.6 = (bf16[1024,128]{1,0:T(8,128)(2,1)S(1)}, bf16[1024,128]{1,0:T(8,128)(2,1)}, u32[]{:S(2)}) copy-start(bf16[1024,128]{1,0:T(8,128)(2,1)} %get-tuple-element.12.key_ref) | copy-start | bytes 786436
  3.9 62.6 %all-to-all-start = ((bf16[64,72,128]{2,1,0:T(8,128)(2,1)}), bf16[64,72,128]{2,1,0:T(8,128)(2,1)}, u32[]{:S(2)}, u32[]{:S(2)}) async-start(bf16[64,72,128]{2,1,0:T(8,128)(2,1)} %get-tuple-element.21), calls=%async_computation | async-start | bytes 2359296 | tf_op jit(solution)/shard_map/all_to_all | solution.py:301
  30.9 0.7 %copy-start = (bf16[128,1024]{1,0:T(8,128)(2,1)}, bf16[128,1024]{1,0:T(8,128)(2,1)S(1)}, u32[]{:S(2)}) copy-start(bf16[128,1024]{1,0:T(8,128)(2,1)S(1)} %get-tuple-element.20.refs_7_) | copy-start | bytes 786436
  31.6 16.0 %collective-permute-start = (bf16[128,1024]{1,0:T(8,128)(2,1)S(1)}, bf16[128,1024]{1,0:T(8,128)(2,1)S(1)}, u32[]{:S(2)}, u32[]{:S(2)}) collective-permute-start(bf16[128,1024]{1,0:T(8,128)(2,1)S(1)} %get-tuple-element.13), channel_id=1, source_target_pairs={{0,2},{1,3},{2,4},{3,5},{4,6},{5,7},{6,0},{7,1},{8,10},{9,11},{10,... | collective-permute-start | bytes 786440 | tf_op jit(solution)/shard_map/ppermute | solution.py:316
  34.7 16.5 %collective-permute-start.1 = (bf16[128,1024]{1,0:T(8,128)(2,1)S(1)}, bf16[128,1024]{1,0:T(8,128)(2,1)S(1)}, u32[]{:S(2)}, u32[]{:S(2)}) collective-permute-start(bf16[128,1024]{1,0:T(8,128)(2,1)S(1)} %get-tuple-element.14), channel_id=1, source_target_pairs={{0,6},{1,7},{2,0},{3,1},{4,2},{5,3},{6,4},{7,5},{8,14},{9,15},{10,... | collective-permute-start | bytes 786440 | tf_op jit(solution)/shard_map/ppermute | solution.py:316
  36.9 18.1 %collective-permute-start.2 = (bf16[128,1024]{1,0:T(8,128)(2,1)}, bf16[128,1024]{1,0:T(8,128)(2,1)S(1)}, u32[]{:S(2)}, u32[]{:S(2)}) collective-permute-start(bf16[128,1024]{1,0:T(8,128)(2,1)} %get-tuple-element.15), channel_id=1, source_target_pairs={{0,4},{1,5},{2,6},{3,7},{4,0},{5,1},{6,2},{7,3},{8,12},{9,13},{10,... | collective-permute-start | bytes 786440 | tf_op jit(solution)/shard_map/ppermute | solution.py:316
  40.6 14.3 %collective-permute-start.3 = (bf16[128,1024]{1,0:T(8,128)(2,1)}, bf16[128,1024]{1,0:T(8,128)(2,1)S(1)}, u32[]{:S(2)}, u32[]{:S(2)}) collective-permute-start(bf16[128,1024]{1,0:T(8,128)(2,1)} %get-tuple-element.16), channel_id=1, source_target_pairs={{0,3},{1,2},{2,5},{3,4},{4,7},{5,6},{6,1},{7,0},{8,11},{9,10},{10,... | collective-permute-start | bytes 786440 | tf_op jit(solution)/shard_map/ppermute | solution.py:316
  45.3 11.8 %collective-permute-start.4 = (bf16[128,1024]{1,0:T(8,128)(2,1)}, bf16[128,1024]{1,0:T(8,128)(2,1)S(1)}, u32[]{:S(2)}, u32[]{:S(2)}) collective-permute-start(bf16[128,1024]{1,0:T(8,128)(2,1)} %get-tuple-element.17), channel_id=1, source_target_pairs={{0,7},{1,6},{2,1},{3,0},{4,3},{5,2},{6,5},{7,4},{8,15},{9,14},{10,... | collective-permute-start | bytes 786440 | tf_op jit(solution)/shard_map/ppermute | solution.py:316
  47.6 15.9 %copy-start.8 = (bf16[128,1024]{1,0:T(8,128)(2,1)}, bf16[128,1024]{1,0:T(8,128)(2,1)S(1)}, u32[]{:S(2)}) copy-start(bf16[128,1024]{1,0:T(8,128)(2,1)S(1)} %collective-permute-done.refs_0_) | copy-start | bytes 786436
  47.6 14.5 %collective-permute-start.5 = (bf16[128,1024]{1,0:T(8,128)(2,1)S(1)}, bf16[128,1024]{1,0:T(8,128)(2,1)S(1)}, u32[]{:S(2)}, u32[]{:S(2)}) collective-permute-start(bf16[128,1024]{1,0:T(8,128)(2,1)S(1)} %get-tuple-element.18), channel_id=1, source_target_pairs={{0,5},{1,4},{2,7},{3,6},{4,1},{5,0},{6,3},{7,2},{8,13},{9,12},{10,... | collective-permute-start | bytes 786440 | tf_op jit(solution)/shard_map/ppermute | solution.py:316
  51.2 0.7 %copy-start.9 = (bf16[128,1024]{1,0:T(8,128)(2,1)}, bf16[128,1024]{1,0:T(8,128)(2,1)S(1)}, u32[]{:S(2)}) copy-start(bf16[128,1024]{1,0:T(8,128)(2,1)S(1)} %collective-permute-done.1.refs_1_) | copy-start | bytes 786436
  51.9 10.2 %collective-permute-start.6 = (bf16[128,1024]{1,0:T(8,128)(2,1)S(1)}, bf16[128,1024]{1,0:T(8,128)(2,1)S(1)}, u32[]{:S(2)}, u32[]{:S(2)}) collective-permute-start(bf16[128,1024]{1,0:T(8,128)(2,1)S(1)} %get-tuple-element.19), channel_id=1, source_target_pairs={{0,1},{1,0},{2,3},{3,2},{4,5},{5,4},{6,7},{7,6},{8,9},{9,8},{10,11... | collective-permute-start | bytes 786440 | tf_op jit(solution)/shard_map/ppermute | solution.py:316
  55.0 7.2 %copy-start.10 = (bf16[128,1024]{1,0:T(8,128)(2,1)}, bf16[128,1024]{1,0:T(8,128)(2,1)S(1)}, u32[]{:S(2)}) copy-start(bf16[128,1024]{1,0:T(8,128)(2,1)S(1)} %collective-permute-done.2.refs_2_) | copy-start | bytes 786436
  55.0 7.2 %copy-start.11 = (bf16[128,1024]{1,0:T(8,128)(2,1)}, bf16[128,1024]{1,0:T(8,128)(2,1)S(1)}, u32[]{:S(2)}) copy-start(bf16[128,1024]{1,0:T(8,128)(2,1)S(1)} %collective-permute-done.3.refs_3_) | copy-start | bytes 786436
  57.1 5.0 %copy-start.12 = (bf16[128,1024]{1,0:T(8,128)(2,1)}, bf16[128,1024]{1,0:T(8,128)(2,1)S(1)}, u32[]{:S(2)}) copy-start(bf16[128,1024]{1,0:T(8,128)(2,1)S(1)} %collective-permute-done.4.refs_4_) | copy-start | bytes 786436
  62.1 0.7 copy-start.13
  62.8 0.7 copy-start.14

commit v2 on v1

--- a/solution.py
+++ b/solution.py
@@ -21,13 +21,13 @@
 GROUPS = 64
 SLOTS = 2 * GROUPS
 CHIPS = 4
-BATCH = 8
+BATCHES = (8,)
 EPS = 1e-06
 LABEL_ROWS = 8
 LETTER = 4 * PAGE + LABEL_ROWS
 NEG = -1e30
 SCALE = HD**-0.5 * np.log2(np.e)
-STEPS = ((1, 0), (3, 0), (2, 0), (1, 1), (3, 1), (2, 1), (0, 1))
+STEPS = ((1, 0), (3, 0), (2, 0), (1, 1), (3, 1), (2, 1), (0, 1), (0, 0))
 
 
 def rope_tables():
@@ -37,6 +37,14 @@
     cosine = np.concatenate([np.cos(angles)] * 2, axis=1)
     sine = np.concatenate([-np.sin(angles), np.sin(angles)], axis=1)
     return cosine.astype(np.float32), sine.astype(np.float32)
+
+
+def target_of(me, step, flip):
+    return ((((me >> 1) + step) & (CHIPS - 1)) << 1) | ((me & 1) ^ flip)
+
+
+def source_of(me, step, flip):
+    return target_of(me, CHIPS - step, flip)
 
 
 def seq_ends(traj_ref):
@@ -92,12 +100,14 @@
 
 
 def attend_kernel(
-    block_ref, traj_ref, query_ref, key_ref, value_ref, gain_ref, cos_ref, sin_ref, *refs
+    steps, me_ref, traj_ref, query_ref, key_ref, value_ref, gain_ref, cos_ref, sin_ref, *refs
 ):
-    for index, out_ref in enumerate(refs[:-4]):
+    out_refs, next_ref, scratch = refs[: len(steps)], refs[len(steps)], refs[len(steps) + 1 :]
+    next_ref[0] = me_ref[0]
+    for (step, flip), out_ref in zip(steps, out_refs):
         attend_block(
-            block_ref[index], traj_ref, query_ref, key_ref, value_ref, gain_ref, cos_ref, sin_ref,
-            out_ref, *refs[-4:],
+            target_of(me_ref[0], step, flip), traj_ref, query_ref, key_ref, value_ref, gain_ref,
+            cos_ref, sin_ref, out_ref, *scratch,
         )
 
 
@@ -121,12 +131,8 @@
     for head in range(HEADS):
         raw = query_ref[rows, head * HD : (head + 1) * HD]
         entries = raw.astype(jnp.float32)
-        square = entries * entries
-        upper = square.astype(jnp.bfloat16)
-        lower = (square - upper.astype(jnp.float32)).astype(jnp.bfloat16)
-        total_square = jnp.dot(
-            jnp.concatenate([upper, lower], axis=1), ones, preferred_element_type=jnp.float32
-        )
+        square = (entries * entries).astype(jnp.bfloat16)
+        total_square = jnp.dot(square, ones[:HD], preferred_element_type=jnp.float32)
         turned = jnp.dot(raw, turn, preferred_element_type=jnp.float32)
         mixed = entries * cos_rows[...] + turned * sin_rows[...]
         scaled = mixed * lax.rsqrt(total_square * (1.0 / HD) + EPS)
@@ -171,28 +177,25 @@
         ).astype(jnp.bfloat16)
 
 
-def assemble_kernel(source_ref, *refs):
-    count = (len(refs) - 3) // 2
-    pieces, out_ref = refs[:count], refs[count]
-    held, in_sems, out_sems = refs[count + 1 : count + 1 + count], refs[-2], refs[-1]
-    loads, stores = [], []
-    for index, piece in enumerate(pieces):
+def assemble_kernel(me_ref, *refs):
+    pieces, out_ref, sems = refs[:-2], refs[-2], refs[-1]
+    copies = []
+    for index, (piece, (step, flip)) in enumerate(zip(pieces, STEPS)):
         width = piece.shape[1]
-        columns = pl.ds(pl.multiple_of(source_ref[index] * width, width), width)
-        loads.append(pltpu.make_async_copy(piece, held[index], in_sems.at[index]))
-        stores.append(
-            pltpu.make_async_copy(held[index], out_ref.at[:, columns], out_sems.at[index])
+        start = pl.multiple_of(source_of(me_ref[0], step, flip) * width, width)
+        copies.append(
+            pltpu.make_async_copy(piece, out_ref.at[:, pl.ds(start, width)], sems.at[index])
         )
-    for load in loads:
-        load.start()
-    for load, store in zip(loads, stores):
-        load.wait()
-        store.start()
-    for store in stores:
-        store.wait()
-
-
-def pool_kernel(arrived_ref, pool_ref, label_ref, slot_ref, place_ref, sem):
+    for copy in copies:
+        copy.start()
+    for copy in copies:
+        copy.wait()
+
+
+def pool_kernel(source_ref, pool_ref, arrived_ref, label_ref, slot_ref, place_ref, sem):
+    load = pltpu.make_async_copy(source_ref, arrived_ref, sem)
+    load.start()
+    load.wait()
     lane = lax.broadcasted_iota(jnp.int32, (LABEL_ROWS, HD), 1) // 2
     labels = jnp.zeros((LABEL_ROWS, HD), jnp.float32)
     for group in range(GROUPS):
@@ -216,7 +219,9 @@
 VMEM = pl.BlockSpec(memory_space=pltpu.VMEM)
 SMEM = pl.BlockSpec(memory_space=pltpu.SMEM)
 ANY = pl.BlockSpec(memory_space=pl.ANY)
+HBM = pl.BlockSpec(memory_space=pltpu.HBM)
 ATTEND_VMEM = 12 << 20
+TAIL_VMEM = 8 << 20
 PARAMS = pltpu.CompilerParams(vmem_limit_bytes=63 << 20)
 
 
@@ -240,12 +245,13 @@
     )(traj, dest, table, key_proj, value_proj, gain, cosine, sine)
 
 
-def attend(blocks, traj, query_proj, ready, value_proj, gain, cosine, sine):
+def attend(steps, me, traj, query_proj, ready, value_proj, gain, cosine, sine):
     return pl.pallas_call(
-        attend_kernel,
-        out_shape=[jax.ShapeDtypeStruct((BLOCK, HEADS * HD), jnp.bfloat16)] * len(blocks),
+        functools.partial(attend_kernel, steps),
+        out_shape=[jax.ShapeDtypeStruct((BLOCK, HEADS * HD), jnp.bfloat16)] * len(steps)
+        + [jax.ShapeDtypeStruct((1,), jnp.int32)],
         in_specs=[SMEM] * 2 + [VMEM] * 6,
-        out_specs=[VMEM] * len(blocks),
+        out_specs=[VMEM] * len(steps) + [SMEM],
         scratch_shapes=[
             pltpu.VMEM((BLOCK, HD), jnp.float32),
             pltpu.VMEM((BLOCK, HD), jnp.float32),
@@ -253,39 +259,39 @@
             pltpu.VMEM((HEADS * BLOCK, 2 * HD), jnp.float32),
         ],
         compiler_params=pltpu.CompilerParams(vmem_limit_bytes=ATTEND_VMEM),
-        cost_estimate=cost(len(blocks) * 400 * 10**6, 4 << 20),
+        cost_estimate=cost(len(steps) * 400 * 10**6, 4 << 20),
         name="attend",
-    )(jnp.stack(blocks), traj, query_proj, ready, value_proj, gain, cosine, sine)
-
-
-def assemble(sources, pieces):
+    )(me, traj, query_proj, ready, value_proj, gain, cosine, sine)
+
+
+def assemble(me, pieces):
     rows, width = pieces[0].shape
     return pl.pallas_call(
         assemble_kernel,
         out_shape=jax.ShapeDtypeStruct((rows, width * len(pieces)), jnp.bfloat16),
-        in_specs=[SMEM] + [ANY] * len(pieces),
+        in_specs=[SMEM] + [VMEM] * len(pieces),
         out_specs=ANY,
-        scratch_shapes=[pltpu.VMEM(piece.shape, piece.dtype) for piece in pieces]
-        + [pltpu.SemaphoreType.DMA((len(pieces),))] * 2,
-        compiler_params=PARAMS,
+        scratch_shapes=[pltpu.SemaphoreType.DMA((len(pieces),))],
+        compiler_params=pltpu.CompilerParams(vmem_limit_bytes=TAIL_VMEM),
         cost_estimate=cost(10**6, 4 << 20),
         name="assemble",
-    )(sources, *pieces)
+    )(me, *pieces)
 
 
 def fill_pool(arrived):
     return pl.pallas_call(
         pool_kernel,
         out_shape=jax.ShapeDtypeStruct((PAGES, PAGE, 2 * HD), jnp.bfloat16),
-        in_specs=[VMEM],
+        in_specs=[HBM],
         out_specs=VMEM,
         scratch_shapes=[
+            pltpu.VMEM(arrived.shape, arrived.dtype),
             pltpu.VMEM((LABEL_ROWS, HD), jnp.int32),
             pltpu.SMEM((LABEL_ROWS, HD), jnp.int32),
             pltpu.SMEM((PAGES + 1,), jnp.int32),
             pltpu.SemaphoreType.DMA,
         ],
-        compiler_params=PARAMS,
+        compiler_params=pltpu.CompilerParams(vmem_limit_bytes=TAIL_VMEM),
         cost_estimate=cost(10**6, 2 << 20),
         name="pool",
     )(arrived)
@@ -300,21 +306,21 @@
     ready, outbox = prep(traj, dest, table, key_proj, value_proj, key_gain, cosine, sine)
     arrived = lax.all_to_all(outbox, "replica", split_axis=0, concat_axis=0, tiled=True)
 
-    me = lax.axis_index("tensor")
-    chip, core = me // 2, me % 2
-    targets = [(chip + step) % CHIPS * 2 + (core ^ flip) for step, flip in STEPS] + [me]
-    sources = [(chip - step + CHIPS) % CHIPS * 2 + (core ^ flip) for step, flip in STEPS] + [me]
-    pieces = []
-    for begin in range(0, len(targets), BATCH):
-        pieces += attend(
-            targets[begin : begin + BATCH], traj, query_proj, ready, value_proj, query_gain, cosine, sine
-        )
-    for index, (step, flip) in enumerate(STEPS):
-        pairs = [
-            (x * 2 + c, (x + step) % CHIPS * 2 + (c ^ flip)) for x in range(CHIPS) for c in range(2)
-        ]
-        pieces[index] = lax.ppermute(pieces[index], "tensor", pairs)
-    return assemble(jnp.stack(sources), pieces), fill_pool(arrived)
+    me = lax.axis_index("tensor").astype(jnp.int32).reshape(1)
+    pieces, first = [], 0
+    for count in BATCHES:
+        steps = STEPS[first : first + count]
+        *parts, me = attend(steps, me, traj, query_proj, ready, value_proj, query_gain, cosine, sine)
+        for (step, flip), piece in zip(steps, parts):
+            pairs = [
+                (x * 2 + c, (x + step) % CHIPS * 2 + (c ^ flip))
+                for x in range(CHIPS)
+                for c in range(2)
+            ]
+            pieces.append(lax.ppermute(piece, "tensor", pairs) if step or flip else piece)
+        first += count
+    pool, me = lax.optimization_barrier((fill_pool(arrived), me))
+    return assemble(me, pieces), pool
 
 
 def solution(mesh):

time: 70.5 us -> 64.7 us (0.918)
  Pallas kernels: 20.3 us -> 17.8 us
  local copies, waits for them, and re-layouts: 3.52 us -> 1.62 us
  waiting for transfers between devices: 7.14 us -> 6.02 us
    unnamed x30 -> x14, local copies, waits for them, and re-layouts: 2.82 us -> 1.62 us
    ppermute x7, waiting for transfers between devices: 7.14 us -> 6.02 us  [shards(): lax.ppermute(piece, 'tensor', pairs)]
    pallas_call x1, Pallas kernels: 3.06 us -> 1.95 us  [assemble(): pl.pallas_call(assemble_kernel, out_shape=jax.ShapeDtypeStruct((rows, wid...]
    pallas_call x1, Pallas kernels: 3.47 us -> 2.44 us  [fill_pool(): pl.pallas_call(pool_kernel, out_shape=jax.ShapeDtypeStruct((PAGES, PAGE,...]
  transfers between devices with their start and end apart: 8 -> 8, of which waited for: 2 -> 2; matrix products, arithmetic and copies ran while one was open for 1% -> 0% of each run, Pallas kernels for 19% -> 20%
where the time goes in v2:
time: 64.7 us; the launch traced here: 64.3 us
  starting transfers between devices  38 us (59%)
  Pallas kernels  17.8 us (28%)
  waiting for transfers between devices  6.02 us (9%)
  local copies, waits for them, and re-layouts  1.62 us (3%)
  between operations  0.85 us (1%)
    ppermute x7, starting transfers between devices, shards(): lax.ppermute(piece, 'tensor', pairs)  22 us
    all_to_all x1, starting transfers between devices, shards(): lax.all_to_all(outbox, 'replica', split_axis=0, concat_axis=0, tiled=True)  16 us
    pallas_call x1, Pallas kernels, attend(): pl.pallas_call(functools.partial(attend_kernel, steps), out_shape=[jax.Sh...  10.1 us
    ppermute x7, waiting for transfers between devices, shards(): lax.ppermute(piece, 'tensor', pairs)  6.02 us
    pallas_call x1, Pallas kernels, prep(): pl.pallas_call(prep_kernel, out_shape=(jax.ShapeDtypeStruct((ROWS, HD), j...  3.26 us
    pallas_call x1, Pallas kernels, fill_pool(): pl.pallas_call(pool_kernel, out_shape=jax.ShapeDtypeStruct((PAGES, PAGE,...  2.44 us
    pallas_call x1, Pallas kernels, assemble(): pl.pallas_call(assemble_kernel, out_shape=jax.ShapeDtypeStruct((rows, wid...  1.95 us
    unnamed x14, local copies, waits for them, and re-layouts  1.62 us
  transfers between devices with their start and end apart: 8, of which 2 were waited for; matrix products, arithmetic and copies ran while one was open for 0% of the time, Pallas kernels for 20%

profile of v2, /device:TPU:19, one launch (start us, length us, event | category | flops | bytes accessed | tf_op | source)
XLA Modules:
  0.0 64.3 jit_solution(18424819803649840600)
XLA Ops:
  0.6 0.0 copy-start.1
  0.6 0.0 copy-start.2
  0.7 3.3 %prep.1 = (bf16[1024,128]{1,0:T(8,128)(2,1)}, bf16[64,72,128]{2,1,0:T(8,128)(2,1)}) custom-call(s32[4]{0:T(128)} %bitcast.6, s32[64]{0:T(128)} %bitcast.9, s32[64]{0:T(128)} %bitcast.10, bf16[1024,128]{1,0:T(8,128)(2,1)} %key_ref.1, bf16[1024,128]{1,0:T(8,128)(2,1)} %value_ref.3, f32[1,128]{1,0:T(1,128)} %bitcast.11, f32[48,128]{1,0:T(8,128)} %constant.8.clone.cos_ref, ...), custom_call_target="tpu_custom_call" | custom-call | flops 1000000 | bytes 4194304 | tf_op jit(solution)/shard_map/prep/pallas_call | solution.py:233
  3.9 16.0 %all-to-all-start = ((bf16[64,72,128]{2,1,0:T(8,128)(2,1)}), bf16[64,72,128]{2,1,0:T(8,128)(2,1)S(1)}, u32[]{:S(2)}, u32[]{:S(2)}) async-start(bf16[64,72,128]{2,1,0:T(8,128)(2,1)} %get-tuple-element.15), calls=%async_computation | async-start | bytes 2359296 | tf_op jit(solution)/shard_map/all_to_all | solution.py:307
  20.1 0.0 copy-start.4
  20.1 1.6 %copy-done.4 = bf16[1024,1024]{1,0:T(8,128)(2,1)S(1)} copy-done((bf16[1024,1024]{1,0:T(8,128)(2,1)S(1)}, bf16[1024,1024]{1,0:T(8,128)(2,1)}, u32[]{:S(2)}) %copy-start.4) | copy-done | bytes 2097176
  21.7 10.1 %attend.1 = (bf16[128,1024]{1,0:T(8,128)(2,1)S(1)}, bf16[128,1024]{1,0:T(8,128)(2,1)S(1)}, bf16[128,1024]{1,0:T(8,128)(2,1)}, bf16[128,1024]{1,0:T(8,128)(2,1)},...) custom-call(s32[1]{0:T(128)} %bitcast.4.me_ref, ...), custom_call_target="tpu_custom_call" | custom-call | flops 3200000000 | bytes 4194304 | tf_op jit(solution)/shard_map/attend/pallas_call | solution.py:249
  31.8 3.1 %collective-permute-start = (bf16[128,1024]{1,0:T(8,128)(2,1)S(1)}, bf16[128,1024]{1,0:T(8,128)(2,1)S(1)}, u32[]{:S(2)}, u32[]{:S(2)}) collective-permute-start(bf16[128,1024]{1,0:T(8,128)(2,1)S(1)} %get-tuple-element.19), channel_id=1, source_target_pairs={{0,2},{1,3},{2,4},{3,5},{4,6},{5,7},{6,0},{7,1},{8,10},{9,11},{10,... | collective-permute-start | bytes 786440 | tf_op jit(solution)/shard_map/ppermute | solution.py:320
  34.9 2.2 %collective-permute-start.1 = (bf16[128,1024]{1,0:T(8,128)(2,1)S(1)}, bf16[128,1024]{1,0:T(8,128)(2,1)S(1)}, u32[]{:S(2)}, u32[]{:S(2)}) collective-permute-start(bf16[128,1024]{1,0:T(8,128)(2,1)S(1)} %get-tuple-element.20), channel_id=1, source_target_pairs={{0,6},{1,7},{2,0},{3,1},{4,2},{5,3},{6,4},{7,5},{8,14},{9,15},{10,... | collective-permute-start | bytes 786440 | tf_op jit(solution)/shard_map/ppermute | solution.py:320
  37.1 3.7 %collective-permute-start.2 = (bf16[128,1024]{1,0:T(8,128)(2,1)}, bf16[128,1024]{1,0:T(8,128)(2,1)S(1)}, u32[]{:S(2)}, u32[]{:S(2)}) collective-permute-start(bf16[128,1024]{1,0:T(8,128)(2,1)} %get-tuple-element.21), channel_id=1, source_target_pairs={{0,4},{1,5},{2,6},{3,7},{4,0},{5,1},{6,2},{7,3},{8,12},{9,13},{10,... | collective-permute-start | bytes 786440 | tf_op jit(solution)/shard_map/ppermute | solution.py:320
  40.8 4.7 %collective-permute-start.3 = (bf16[128,1024]{1,0:T(8,128)(2,1)}, bf16[128,1024]{1,0:T(8,128)(2,1)S(1)}, u32[]{:S(2)}, u32[]{:S(2)}) collective-permute-start(bf16[128,1024]{1,0:T(8,128)(2,1)} %get-tuple-element.22), channel_id=1, source_target_pairs={{0,3},{1,2},{2,5},{3,4},{4,7},{5,6},{6,1},{7,0},{8,11},{9,10},{10,... | collective-permute-start | bytes 786440 | tf_op jit(solution)/shard_map/ppermute | solution.py:320
  45.5 2.3 %collective-permute-start.4 = (bf16[128,1024]{1,0:T(8,128)(2,1)}, bf16[128,1024]{1,0:T(8,128)(2,1)S(1)}, u32[]{:S(2)}, u32[]{:S(2)}) collective-permute-start(bf16[128,1024]{1,0:T(8,128)(2,1)} %get-tuple-element.23), channel_id=1, source_target_pairs={{0,7},{1,6},{2,1},{3,0},{4,3},{5,2},{6,5},{7,4},{8,15},{9,14},{10,... | collective-permute-start | bytes 786440 | tf_op jit(solution)/shard_map/ppermute | solution.py:320
  47.8 0.0 collective-permute-done.refs_0_
  47.8 3.6 %collective-permute-start.5 = (bf16[128,1024]{1,0:T(8,128)(2,1)}, bf16[128,1024]{1,0:T(8,128)(2,1)S(1)}, u32[]{:S(2)}, u32[]{:S(2)}) collective-permute-start(bf16[128,1024]{1,0:T(8,128)(2,1)} %get-tuple-element.24), channel_id=1, source_target_pairs={{0,5},{1,4},{2,7},{3,6},{4,1},{5,0},{6,3},{7,2},{8,13},{9,12},{10,... | collective-permute-start | bytes 786440 | tf_op jit(solution)/shard_map/ppermute | solution.py:320
  51.4 0.0 collective-permute-done.1.refs_1_
  51.4 2.4 %collective-permute-start.6 = (bf16[128,1024]{1,0:T(8,128)(2,1)S(1)}, bf16[128,1024]{1,0:T(8,128)(2,1)S(1)}, u32[]{:S(2)}, u32[]{:S(2)}) collective-permute-start(bf16[128,1024]{1,0:T(8,128)(2,1)S(1)} %get-tuple-element.25), channel_id=1, source_target_pairs={{0,1},{1,0},{2,3},{3,2},{4,5},{5,4},{6,7},{7,6},{8,9},{9,8},{10,11... | collective-permute-start | bytes 786440 | tf_op jit(solution)/shard_map/ppermute | solution.py:320
  53.8 0.0 all-to-all-done.source_ref
  53.8 2.4 %pool.1 = bf16[64,16,256]{2,1,0:T(8,128)(2,1)} custom-call(bf16[64,72,128]{2,1,0:T(8,128)(2,1)S(1)} %all-to-all-done.source_ref), custom_call_target="tpu_custom_call" | custom-call | flops 1000000 | bytes 2097152 | tf_op jit(solution)/shard_map/pool/pallas_call | solution.py:282
  56.3 0.0 collective-permute-done.2.refs_2_
  56.3 0.0 collective-permute-done.3.refs_3_
  56.3 0.9 %collective-permute-done.4.refs_4_ = bf16[128,1024]{1,0:T(8,128)(2,1)S(1)} collective-permute-done((bf16[128,1024]{1,0:T(8,128)(2,1)}, bf16[128,1024]{1,0:T(8,128)(2,1)S(1)}, u32[]{:S(2)}, u32[]{:S(2)}) %collective-permute-start.4) | collective-permute-done | bytes 262176 | tf_op jit(solution)/shard_map/ppermute | solution.py:320
  57.2 5.1 %collective-permute-done.5.refs_5_ = bf16[128,1024]{1,0:T(8,128)(2,1)S(1)} collective-permute-done((bf16[128,1024]{1,0:T(8,128)(2,1)}, bf16[128,1024]{1,0:T(8,128)(2,1)S(1)}, u32[]{:S(2)}, u32[]{:S(2)}) %collective-permute-start.5) | collective-permute-done | bytes 262176 | tf_op jit(solution)/shard_map/ppermute | solution.py:320
  62.3 0.0 collective-permute-done.6.refs_6_
  62.3 2.0 %assemble.1 = bf16[128,8192]{1,0:T(8,128)(2,1)} custom-call(s32[1]{0:T(128)} %get-tuple-element.18.me_ref, bf16[128,1024]{1,0:T(8,128)(2,1)S(1)} %collective-permute-done.refs_0_, bf16[128,1024]{1,0:T(8,128)(2,1)S(1)} %collective-permute-done.1.refs_1_, bf16[128,1024]{1,0:T(8,128)(2,1)S(1)} %collective-permute-done.2.refs_2_, ...), custom_call_target="tpu_custom_call" | custom-call | flops 1000000 | bytes 4194304 | tf_op jit(solution)/shard_map/assemble/pallas_call | solution.py:269
  (10 shorter events, 0.0 us)
Async XLA Ops:
  0.6 19.4 %copy-start.1 = (f32[48,128]{1,0:T(8,128)S(1)}, f32[48,128]{1,0:T(8,128)}, u32[]{:S(2)}) copy-start(f32[48,128]{1,0:T(8,128)} %constant.9.clone.sin_ref) | copy-start | bytes 73732
  0.6 19.4 %copy-start.2 = (f32[48,128]{1,0:T(8,128)S(1)}, f32[48,128]{1,0:T(8,128)}, u32[]{:S(2)}) copy-start(f32[48,128]{1,0:T(8,128)} %constant.8.clone.cos_ref) | copy-start | bytes 73732
  0.7 19.4 %copy-start = (bf16[1024,128]{1,0:T(8,128)(2,1)S(1)}, bf16[1024,128]{1,0:T(8,128)(2,1)}, u32[]{:S(2)}) copy-start(bf16[1024,128]{1,0:T(8,128)(2,1)} %value_ref.3) | copy-start | bytes 786436
  0.7 19.4 %copy-start.3 = (s32[1,4]{1,0:T(1,128)S(1)}, s32[1,4]{1,0:T(1,128)}, u32[]{:S(2)}) copy-start(s32[1,4]{1,0:T(1,128)} %param.13) | copy-start | bytes 52
  0.7 19.4 %copy-start.6 = (f32[128]{0:T(128)S(1)}, f32[128]{0:T(128)}, u32[]{:S(2)}) copy-start(f32[128]{0:T(128)} %param.16) | copy-start | bytes 1540
  3.9 16.1 %copy-start.5 = (bf16[1024,128]{1,0:T(8,128)(2,1)S(1)}, bf16[1024,128]{1,0:T(8,128)(2,1)}, u32[]{:S(2)}) copy-start(bf16[1024,128]{1,0:T(8,128)(2,1)} %get-tuple-element.16.key_ref) | copy-start | bytes 786436
  3.9 49.9 %all-to-all-start = ((bf16[64,72,128]{2,1,0:T(8,128)(2,1)}), bf16[64,72,128]{2,1,0:T(8,128)(2,1)S(1)}, u32[]{:S(2)}, u32[]{:S(2)}) async-start(bf16[64,72,128]{2,1,0:T(8,128)(2,1)} %get-tuple-element.15), calls=%async_computation | async-start | bytes 2359296 | tf_op jit(solution)/shard_map/all_to_all | solution.py:307
  20.1 1.6 %copy-start.4 = (bf16[1024,1024]{1,0:T(8,128)(2,1)S(1)}, bf16[1024,1024]{1,0:T(8,128)(2,1)}, u32[]{:S(2)}) copy-start(bf16[1024,1024]{1,0:T(8,128)(2,1)} %query_ref.1) | copy-start | bytes 6291460
  31.8 16.0 %collective-permute-start = (bf16[128,1024]{1,0:T(8,128)(2,1)S(1)}, bf16[128,1024]{1,0:T(8,128)(2,1)S(1)}, u32[]{:S(2)}, u32[]{:S(2)}) collective-permute-start(bf16[128,1024]{1,0:T(8,128)(2,1)S(1)} %get-tuple-element.19), channel_id=1, source_target_pairs={{0,2},{1,3},{2,4},{3,5},{4,6},{5,7},{6,0},{7,1},{8,10},{9,11},{10,... | collective-permute-start | bytes 786440 | tf_op jit(solution)/shard_map/ppermute | solution.py:320
  34.9 16.5 %collective-permute-start.1 = (bf16[128,1024]{1,0:T(8,128)(2,1)S(1)}, bf16[128,1024]{1,0:T(8,128)(2,1)S(1)}, u32[]{:S(2)}, u32[]{:S(2)}) collective-permute-start(bf16[128,1024]{1,0:T(8,128)(2,1)S(1)} %get-tuple-element.20), channel_id=1, source_target_pairs={{0,6},{1,7},{2,0},{3,1},{4,2},{5,3},{6,4},{7,5},{8,14},{9,15},{10,... | collective-permute-start | bytes 786440 | tf_op jit(solution)/shard_map/ppermute | solution.py:320
  37.1 19.2 %collective-permute-start.2 = (bf16[128,1024]{1,0:T(8,128)(2,1)}, bf16[128,1024]{1,0:T(8,128)(2,1)S(1)}, u32[]{:S(2)}, u32[]{:S(2)}) collective-permute-start(bf16[128,1024]{1,0:T(8,128)(2,1)} %get-tuple-element.21), channel_id=1, source_target_pairs={{0,4},{1,5},{2,6},{3,7},{4,0},{5,1},{6,2},{7,3},{8,12},{9,13},{10,... | collective-permute-start | bytes 786440 | tf_op jit(solution)/shard_map/ppermute | solution.py:320
  40.8 15.5 %collective-permute-start.3 = (bf16[128,1024]{1,0:T(8,128)(2,1)}, bf16[128,1024]{1,0:T(8,128)(2,1)S(1)}, u32[]{:S(2)}, u32[]{:S(2)}) collective-permute-start(bf16[128,1024]{1,0:T(8,128)(2,1)} %get-tuple-element.22), channel_id=1, source_target_pairs={{0,3},{1,2},{2,5},{3,4},{4,7},{5,6},{6,1},{7,0},{8,11},{9,10},{10,... | collective-permute-start | bytes 786440 | tf_op jit(solution)/shard_map/ppermute | solution.py:320
  45.5 11.7 %collective-permute-start.4 = (bf16[128,1024]{1,0:T(8,128)(2,1)}, bf16[128,1024]{1,0:T(8,128)(2,1)S(1)}, u32[]{:S(2)}, u32[]{:S(2)}) collective-permute-start(bf16[128,1024]{1,0:T(8,128)(2,1)} %get-tuple-element.23), channel_id=1, source_target_pairs={{0,7},{1,6},{2,1},{3,0},{4,3},{5,2},{6,5},{7,4},{8,15},{9,14},{10,... | collective-permute-start | bytes 786440 | tf_op jit(solution)/shard_map/ppermute | solution.py:320
  47.8 14.5 %collective-permute-start.5 = (bf16[128,1024]{1,0:T(8,128)(2,1)}, bf16[128,1024]{1,0:T(8,128)(2,1)S(1)}, u32[]{:S(2)}, u32[]{:S(2)}) collective-permute-start(bf16[128,1024]{1,0:T(8,128)(2,1)} %get-tuple-element.24), channel_id=1, source_target_pairs={{0,5},{1,4},{2,7},{3,6},{4,1},{5,0},{6,3},{7,2},{8,13},{9,12},{10,... | collective-permute-start | bytes 786440 | tf_op jit(solution)/shard_map/ppermute | solution.py:320
  51.4 10.9 %collective-permute-start.6 = (bf16[128,1024]{1,0:T(8,128)(2,1)S(1)}, bf16[128,1024]{1,0:T(8,128)(2,1)S(1)}, u32[]{:S(2)}, u32[]{:S(2)}) collective-permute-start(bf16[128,1024]{1,0:T(8,128)(2,1)S(1)} %get-tuple-element.25), channel_id=1, source_target_pairs={{0,1},{1,0},{2,3},{3,2},{4,5},{5,4},{6,7},{7,6},{8,9},{9,8},{10,11... | collective-permute-start | bytes 786440 | tf_op jit(solution)/shard_map/ppermute | solution.py:320

commit v3 on v2

--- a/solution.py
+++ b/solution.py
@@ -27,7 +27,7 @@
 LETTER = 4 * PAGE + LABEL_ROWS
 NEG = -1e30
 SCALE = HD**-0.5 * np.log2(np.e)
-STEPS = ((1, 0), (3, 0), (2, 0), (1, 1), (3, 1), (2, 1), (0, 1), (0, 0))
+STEPS = ((2, 0), (2, 1), (1, 0), (3, 0), (1, 1), (3, 1), (0, 1), (0, 0))
 
 
 def rope_tables():
@@ -305,6 +305,7 @@
     query_gain, key_gain = query_gain[None, :], key_gain[None, :]
     ready, outbox = prep(traj, dest, table, key_proj, value_proj, key_gain, cosine, sine)
     arrived = lax.all_to_all(outbox, "replica", split_axis=0, concat_axis=0, tiled=True)
+    arrived = pltpu.with_memory_space_constraint(arrived, pltpu.HBM)
 
     me = lax.axis_index("tensor").astype(jnp.int32).reshape(1)
     pieces, first = [], 0

time: 64.7 us -> 63.5 us (0.981)
  the two profiles are of different devices: /device:TPU:19 before, /device:TPU:1 now
where the time goes in v3:
time: 63.5 us; the launch traced here: 63 us
  starting transfers between devices  41 us (65%)
  Pallas kernels  18.7 us (29%)
  waiting for transfers between devices  1.45 us (2%)
  local copies, waits for them, and re-layouts  0.98 us (2%)
  between operations  0.85 us (1%)
    ppermute x7, starting transfers between devices, shards(): lax.ppermute(piece, 'tensor', pairs)  23.5 us
    all_to_all x1, starting transfers between devices, shards(): lax.all_to_all(outbox, 'replica', split_axis=0, concat_axis=0, tiled=True)  17.5 us
    pallas_call x1, Pallas kernels, attend(): pl.pallas_call(functools.partial(attend_kernel, steps), out_shape=[jax.Sh...  10 us
    pallas_call x1, Pallas kernels, fill_pool(): pl.pallas_call(pool_kernel, out_shape=jax.ShapeDtypeStruct((PAGES, PAGE,...  3.47 us
    pallas_call x1, Pallas kernels, prep(): pl.pallas_call(prep_kernel, out_shape=(jax.ShapeDtypeStruct((ROWS, HD), j...  3.26 us
    pallas_call x1, Pallas kernels, assemble(): pl.pallas_call(assemble_kernel, out_shape=jax.ShapeDtypeStruct((rows, wid...  2 us
    ppermute x7, waiting for transfers between devices, shards(): lax.ppermute(piece, 'tensor', pairs)  1.44 us
  transfers between devices with their start and end apart: 8, of which 1 were waited for; matrix products, arithmetic and copies ran while one was open for 0% of the time, Pallas kernels for 21%

profile of v3, /device:TPU:1, one launch (start us, length us, event | category | flops | bytes accessed | tf_op | source)
XLA Modules:
  0.0 63.0 jit_solution(12225303090427601965)
XLA Ops:
  0.6 0.0 copy-start.1
  0.6 0.0 copy-start.2
  0.7 3.3 %prep.1 = (bf16[1024,128]{1,0:T(8,128)(2,1)}, bf16[64,72,128]{2,1,0:T(8,128)(2,1)}) custom-call(s32[4]{0:T(128)} %bitcast.6, s32[64]{0:T(128)} %bitcast.9, s32[64]{0:T(128)} %bitcast.10, bf16[1024,128]{1,0:T(8,128)(2,1)} %key_ref.1, bf16[1024,128]{1,0:T(8,128)(2,1)} %value_ref.3, f32[1,128]{1,0:T(1,128)} %bitcast.11, f32[48,128]{1,0:T(8,128)} %constant.8.clone.cos_ref, ...), custom_call_target="tpu_custom_call" | custom-call | flops 1000000 | bytes 4194304 | tf_op jit(solution)/shard_map/prep/pallas_call | solution.py:233
  3.9 17.5 %all-to-all-start = ((bf16[64,72,128]{2,1,0:T(8,128)(2,1)}), bf16[64,72,128]{2,1,0:T(8,128)(2,1)}, u32[]{:S(2)}, u32[]{:S(2)}) async-start(bf16[64,72,128]{2,1,0:T(8,128)(2,1)} %get-tuple-element.15), calls=%async_computation | async-start | bytes 2359296 | tf_op jit(solution)/shard_map/all_to_all | solution.py:307
  21.5 0.0 copy-start.5
  21.5 0.9 %copy-done.5 = bf16[1024,128]{1,0:T(8,128)(2,1)S(1)} copy-done((bf16[1024,128]{1,0:T(8,128)(2,1)S(1)}, bf16[1024,128]{1,0:T(8,128)(2,1)}, u32[]{:S(2)}) %copy-start.5) | copy-done | bytes 262168
  22.5 10.0 %attend.1 = (bf16[128,1024]{1,0:T(8,128)(2,1)S(1)}, bf16[128,1024]{1,0:T(8,128)(2,1)S(1)}, bf16[128,1024]{1,0:T(8,128)(2,1)}, bf16[128,1024]{1,0:T(8,128)(2,1)},...) custom-call(s32[1]{0:T(128)} %bitcast.4.me_ref, ...), custom_call_target="tpu_custom_call" | custom-call | flops 3200000000 | bytes 4194304 | tf_op jit(solution)/shard_map/attend/pallas_call | solution.py:249
  32.5 4.6 %collective-permute-start = (bf16[128,1024]{1,0:T(8,128)(2,1)S(1)}, bf16[128,1024]{1,0:T(8,128)(2,1)S(1)}, u32[]{:S(2)}, u32[]{:S(2)}) collective-permute-start(bf16[128,1024]{1,0:T(8,128)(2,1)S(1)} %get-tuple-element.19), channel_id=1, source_target_pairs={{0,4},{1,5},{2,6},{3,7},{4,0},{5,1},{6,2},{7,3},{8,12},{9,13},{10,... | collective-permute-start | bytes 786440 | tf_op jit(solution)/shard_map/ppermute | solution.py:321
  37.1 3.3 %collective-permute-start.1 = (bf16[128,1024]{1,0:T(8,128)(2,1)S(1)}, bf16[128,1024]{1,0:T(8,128)(2,1)S(1)}, u32[]{:S(2)}, u32[]{:S(2)}) collective-permute-start(bf16[128,1024]{1,0:T(8,128)(2,1)S(1)} %get-tuple-element.20), channel_id=1, source_target_pairs={{0,5},{1,4},{2,7},{3,6},{4,1},{5,0},{6,3},{7,2},{8,13},{9,12},{10,... | collective-permute-start | bytes 786440 | tf_op jit(solution)/shard_map/ppermute | solution.py:321
  40.4 3.1 %collective-permute-start.2 = (bf16[128,1024]{1,0:T(8,128)(2,1)}, bf16[128,1024]{1,0:T(8,128)(2,1)S(1)}, u32[]{:S(2)}, u32[]{:S(2)}) collective-permute-start(bf16[128,1024]{1,0:T(8,128)(2,1)} %get-tuple-element.21), channel_id=1, source_target_pairs={{0,2},{1,3},{2,4},{3,5},{4,6},{5,7},{6,0},{7,1},{8,10},{9,11},{10,... | collective-permute-start | bytes 786440 | tf_op jit(solution)/shard_map/ppermute | solution.py:321
  43.5 3.4 %collective-permute-start.3 = (bf16[128,1024]{1,0:T(8,128)(2,1)}, bf16[128,1024]{1,0:T(8,128)(2,1)S(1)}, u32[]{:S(2)}, u32[]{:S(2)}) collective-permute-start(bf16[128,1024]{1,0:T(8,128)(2,1)} %get-tuple-element.22), channel_id=1, source_target_pairs={{0,6},{1,7},{2,0},{3,1},{4,2},{5,3},{6,4},{7,5},{8,14},{9,15},{10,... | collective-permute-start | bytes 786440 | tf_op jit(solution)/shard_map/ppermute | solution.py:321
  46.9 1.9 %collective-permute-start.4 = (bf16[128,1024]{1,0:T(8,128)(2,1)}, bf16[128,1024]{1,0:T(8,128)(2,1)S(1)}, u32[]{:S(2)}, u32[]{:S(2)}) collective-permute-start(bf16[128,1024]{1,0:T(8,128)(2,1)} %get-tuple-element.23), channel_id=1, source_target_pairs={{0,3},{1,2},{2,5},{3,4},{4,7},{5,6},{6,1},{7,0},{8,11},{9,10},{10,... | collective-permute-start | bytes 786440 | tf_op jit(solution)/shard_map/ppermute | solution.py:321
  48.8 0.0 collective-permute-done.refs_0_
  48.8 4.9 %collective-permute-start.5 = (bf16[128,1024]{1,0:T(8,128)(2,1)S(1)}, bf16[128,1024]{1,0:T(8,128)(2,1)S(1)}, u32[]{:S(2)}, u32[]{:S(2)}) collective-permute-start(bf16[128,1024]{1,0:T(8,128)(2,1)S(1)} %get-tuple-element.24), channel_id=1, source_target_pairs={{0,7},{1,6},{2,1},{3,0},{4,3},{5,2},{6,5},{7,4},{8,15},{9,14},{10,... | collective-permute-start | bytes 786440 | tf_op jit(solution)/shard_map/ppermute | solution.py:321
  53.7 0.0 collective-permute-done.1.refs_1_
  53.7 2.4 %collective-permute-start.6 = (bf16[128,1024]{1,0:T(8,128)(2,1)S(1)}, bf16[128,1024]{1,0:T(8,128)(2,1)S(1)}, u32[]{:S(2)}, u32[]{:S(2)}) collective-permute-start(bf16[128,1024]{1,0:T(8,128)(2,1)S(1)} %get-tuple-element.25), channel_id=1, source_target_pairs={{0,1},{1,0},{2,3},{3,2},{4,5},{5,4},{6,7},{7,6},{8,9},{9,8},{10,11... | collective-permute-start | bytes 786440 | tf_op jit(solution)/shard_map/ppermute | solution.py:321
  56.1 0.0 all-to-all-done.source_ref
  56.1 3.5 %pool.1 = bf16[64,16,256]{2,1,0:T(8,128)(2,1)} custom-call(bf16[64,72,128]{2,1,0:T(8,128)(2,1)} %all-to-all-done.source_ref), custom_call_target="tpu_custom_call" | custom-call | flops 1000000 | bytes 2097152 | tf_op jit(solution)/shard_map/pool/pallas_call | solution.py:282
  59.6 0.0 collective-permute-done.2.refs_2_
  59.6 0.0 collective-permute-done.3.refs_3_
  59.6 1.4 %collective-permute-done.4.refs_4_ = bf16[128,1024]{1,0:T(8,128)(2,1)S(1)} collective-permute-done((bf16[128,1024]{1,0:T(8,128)(2,1)}, bf16[128,1024]{1,0:T(8,128)(2,1)S(1)}, u32[]{:S(2)}, u32[]{:S(2)}) %collective-permute-start.4) | collective-permute-done | bytes 262176 | tf_op jit(solution)/shard_map/ppermute | solution.py:321
  61.0 0.0 collective-permute-done.5.refs_5_
  61.0 0.0 collective-permute-done.6.refs_6_
  61.0 2.0 %assemble.1 = bf16[128,8192]{1,0:T(8,128)(2,1)} custom-call(s32[1]{0:T(128)} %get-tuple-element.18.me_ref, bf16[128,1024]{1,0:T(8,128)(2,1)S(1)} %collective-permute-done.refs_0_, bf16[128,1024]{1,0:T(8,128)(2,1)S(1)} %collective-permute-done.1.refs_1_, bf16[128,1024]{1,0:T(8,128)(2,1)S(1)} %collective-permute-done.2.refs_2_, ...), custom_call_target="tpu_custom_call" | custom-call | flops 1000000 | bytes 4194304 | tf_op jit(solution)/shard_map/assemble/pallas_call | solution.py:269
  (10 shorter events, 0.0 us)
Async XLA Ops:
  0.6 20.8 %copy-start.1 = (f32[48,128]{1,0:T(8,128)S(1)}, f32[48,128]{1,0:T(8,128)}, u32[]{:S(2)}) copy-start(f32[48,128]{1,0:T(8,128)} %constant.9.clone.sin_ref) | copy-start | bytes 73732
  0.6 20.8 %copy-start.2 = (f32[48,128]{1,0:T(8,128)S(1)}, f32[48,128]{1,0:T(8,128)}, u32[]{:S(2)}) copy-start(f32[48,128]{1,0:T(8,128)} %constant.8.clone.cos_ref) | copy-start | bytes 73732
  0.7 20.8 %copy-start = (bf16[1024,128]{1,0:T(8,128)(2,1)S(1)}, bf16[1024,128]{1,0:T(8,128)(2,1)}, u32[]{:S(2)}) copy-start(bf16[1024,128]{1,0:T(8,128)(2,1)} %value_ref.3) | copy-start | bytes 786436
  0.7 20.8 %copy-start.3 = (s32[1,4]{1,0:T(1,128)S(1)}, s32[1,4]{1,0:T(1,128)}, u32[]{:S(2)}) copy-start(s32[1,4]{1,0:T(1,128)} %param.13) | copy-start | bytes 52
  0.7 20.8 %copy-start.6 = (f32[128]{0:T(128)S(1)}, f32[128]{0:T(128)}, u32[]{:S(2)}) copy-start(f32[128]{0:T(128)} %param.16) | copy-start | bytes 1540
  3.9 17.6 %copy-start.4 = (bf16[1024,1024]{1,0:T(8,128)(2,1)S(1)}, bf16[1024,1024]{1,0:T(8,128)(2,1)}, u32[]{:S(2)}) copy-start(bf16[1024,1024]{1,0:T(8,128)(2,1)} %query_ref.1) | copy-start | bytes 6291460
  3.9 52.1 %all-to-all-start = ((bf16[64,72,128]{2,1,0:T(8,128)(2,1)}), bf16[64,72,128]{2,1,0:T(8,128)(2,1)}, u32[]{:S(2)}, u32[]{:S(2)}) async-start(bf16[64,72,128]{2,1,0:T(8,128)(2,1)} %get-tuple-element.15), calls=%async_computation | async-start | bytes 2359296 | tf_op jit(solution)/shard_map/all_to_all | solution.py:307
  21.5 1.0 %copy-start.5 = (bf16[1024,128]{1,0:T(8,128)(2,1)S(1)}, bf16[1024,128]{1,0:T(8,128)(2,1)}, u32[]{:S(2)}) copy-start(bf16[1024,128]{1,0:T(8,128)(2,1)} %get-tuple-element.16.key_ref) | copy-start | bytes 786436
  32.5 16.4 %collective-permute-start = (bf16[128,1024]{1,0:T(8,128)(2,1)S(1)}, bf16[128,1024]{1,0:T(8,128)(2,1)S(1)}, u32[]{:S(2)}, u32[]{:S(2)}) collective-permute-start(bf16[128,1024]{1,0:T(8,128)(2,1)S(1)} %get-tuple-element.19), channel_id=1, source_target_pairs={{0,4},{1,5},{2,6},{3,7},{4,0},{5,1},{6,2},{7,3},{8,12},{9,13},{10,... | collective-permute-start | bytes 786440 | tf_op jit(solution)/shard_map/ppermute | solution.py:321
  37.1 16.6 %collective-permute-start.1 = (bf16[128,1024]{1,0:T(8,128)(2,1)S(1)}, bf16[128,1024]{1,0:T(8,128)(2,1)S(1)}, u32[]{:S(2)}, u32[]{:S(2)}) collective-permute-start(bf16[128,1024]{1,0:T(8,128)(2,1)S(1)} %get-tuple-element.20), channel_id=1, source_target_pairs={{0,5},{1,4},{2,7},{3,6},{4,1},{5,0},{6,3},{7,2},{8,13},{9,12},{10,... | collective-permute-start | bytes 786440 | tf_op jit(solution)/shard_map/ppermute | solution.py:321
  40.4 19.2 %collective-permute-start.2 = (bf16[128,1024]{1,0:T(8,128)(2,1)}, bf16[128,1024]{1,0:T(8,128)(2,1)S(1)}, u32[]{:S(2)}, u32[]{:S(2)}) collective-permute-start(bf16[128,1024]{1,0:T(8,128)(2,1)} %get-tuple-element.21), channel_id=1, source_target_pairs={{0,2},{1,3},{2,4},{3,5},{4,6},{5,7},{6,0},{7,1},{8,10},{9,11},{10,... | collective-permute-start | bytes 786440 | tf_op jit(solution)/shard_map/ppermute | solution.py:321
  43.5 16.1 %collective-permute-start.3 = (bf16[128,1024]{1,0:T(8,128)(2,1)}, bf16[128,1024]{1,0:T(8,128)(2,1)S(1)}, u32[]{:S(2)}, u32[]{:S(2)}) collective-permute-start(bf16[128,1024]{1,0:T(8,128)(2,1)} %get-tuple-element.22), channel_id=1, source_target_pairs={{0,6},{1,7},{2,0},{3,1},{4,2},{5,3},{6,4},{7,5},{8,14},{9,15},{10,... | collective-permute-start | bytes 786440 | tf_op jit(solution)/shard_map/ppermute | solution.py:321
  46.9 14.1 %collective-permute-start.4 = (bf16[128,1024]{1,0:T(8,128)(2,1)}, bf16[128,1024]{1,0:T(8,128)(2,1)S(1)}, u32[]{:S(2)}, u32[]{:S(2)}) collective-permute-start(bf16[128,1024]{1,0:T(8,128)(2,1)} %get-tuple-element.23), channel_id=1, source_target_pairs={{0,3},{1,2},{2,5},{3,4},{4,7},{5,6},{6,1},{7,0},{8,11},{9,10},{10,... | collective-permute-start | bytes 786440 | tf_op jit(solution)/shard_map/ppermute | solution.py:321
  48.8 12.2 %collective-permute-start.5 = (bf16[128,1024]{1,0:T(8,128)(2,1)S(1)}, bf16[128,1024]{1,0:T(8,128)(2,1)S(1)}, u32[]{:S(2)}, u32[]{:S(2)}) collective-permute-start(bf16[128,1024]{1,0:T(8,128)(2,1)S(1)} %get-tuple-element.24), channel_id=1, source_target_pairs={{0,7},{1,6},{2,1},{3,0},{4,3},{5,2},{6,5},{7,4},{8,15},{9,14},{10,... | collective-permute-start | bytes 786440 | tf_op jit(solution)/shard_map/ppermute | solution.py:321
  53.7 7.3 %collective-permute-start.6 = (bf16[128,1024]{1,0:T(8,128)(2,1)S(1)}, bf16[128,1024]{1,0:T(8,128)(2,1)S(1)}, u32[]{:S(2)}, u32[]{:S(2)}) collective-permute-start(bf16[128,1024]{1,0:T(8,128)(2,1)S(1)} %get-tuple-element.25), channel_id=1, source_target_pairs={{0,1},{1,0},{2,3},{3,2},{4,5},{5,4},{6,7},{7,6},{8,9},{9,8},{10,11... | collective-permute-start | bytes 786440 | tf_op jit(solution)/shard_map/ppermute | solution.py:321
